TPU v7x, 128 devices: a whole 4x4x4 slice. The times are simulated.
128 devices in a mesh: row: 4 (over z_lo, core), basis: 8 (over z_hi, y), rep: 4 (over x).
Axes of the slice: x: 4, y: 4, z: 4 (z_hi: 2, z_lo: 2; z = z_hi * 2 + z_lo), core: 2. Of those that a mesh axis runs over, the one named last changes fastest.
Arguments:
- blocks: float32 [3072, 7, 128, 128], P(('row', 'basis', 'rep')), as said below
- pattern: int32 [3072, 7], P(('row', 'basis', 'rep')), may hold values from 0 to 3071, as said below
- counts: int32 [3072], P(('row', 'basis', 'rep')), may hold values from 1 to 7, as said below
- stored: float32 [512, 393216], P(None, ('row', 'basis', 'rep')), as said below
- start_block: float32 [64, 393216], P(None, ('row', 'basis', 'rep')), may hold values from -6 to 6, as said below
Outputs:
- diagonal_blocks: float32 [2, 64, 64], replicated
- coupling_blocks: float32 [2, 64, 64], replicated
- last_block: float32 [64, 393216], P(None, ('row', 'basis', 'rep'))
Inputs may be any that keep to these rules, and one draw needn't show every extreme that they name: `pattern`: the first counts[i] entries of row block i are distinct column blocks j with (j - i) mod 3072 at most 24 or at least 3048; the used entries are symmetric (i uses j exactly when j uses i); the other entries are column blocks within the same reach. `counts`: the number of used slots of each row block; some row block uses all 7. The used blocks form a symmetric matrix: the block of row block i at column block j is the transpose of that of j at i. `stored`: real entries of order one over the square root of 393216. `start_block`: real entries of order one.
All inputs are finite; a program needn't handle non-finite values.
Results may differ from a plain program's by a relative error of at most 0.00016.
Values sent between devices are 32-bit elements; how exact they have to be, the bound alone decides.
No kernel may reach another device: no remote copies, remote signals or barrier semaphores. Data moves between devices by JAX's collectives and lax.ppermute only.
A program may use at most 128 MiB of HBM per device.

v0:
```python
import functools
import math

import jax
import jax.numpy as jnp
from jax import lax
from jax.experimental import pallas as pl
from jax.experimental.pallas import tpu as pltpu
from jax.sharding import PartitionSpec as P

AXES = ("row", "basis", "rep")
HIGH = lax.Precision.HIGH
FULL = lax.Precision.HIGHEST
F32 = jnp.float32
BF16 = jnp.bfloat16
RB = 2
TILE = 768
VMEM_LIMIT = 48 * 1024 * 1024


def dot_nt(a, b, precision=FULL):
    return lax.dot_general(a, b, (((1,), (1,)), ((), ())), precision=precision, preferred_element_type=F32)


def dot_tn(a, b, precision=FULL):
    return lax.dot_general(a, b, (((0,), (0,)), ((), ())), precision=precision, preferred_element_type=F32)


def dot_nn(a, b, precision=FULL):
    return lax.dot_general(a, b, (((1,), (0,)), ((), ())), precision=precision, preferred_element_type=F32)


def bdot(a, b):
    return jnp.dot(a, b, preferred_element_type=F32)


def total(x):
    n = lax.axis_size(AXES)
    parts = lax.all_to_all(x.reshape(n, x.size // n), AXES, 0, 0, tiled=True)
    mine = jnp.sum(parts, axis=0)
    out = lax.all_to_all(jnp.broadcast_to(mine[None], parts.shape), AXES, 0, 0, tiled=True)
    return out.reshape(x.shape)


def split(x):
    hi = x.astype(BF16)
    lo = (x - hi.astype(F32)).astype(BF16)
    return hi, lo


def turned(x):
    hi = x.astype(BF16).astype(F32)
    return jnp.concatenate([hi, x - hi], axis=0).T.astype(BF16)


def apply_kernel(cols, blocks, stored, left, mid, right, prev, u_out, m_out, pieces, acc, accw, *, nbd):
    step = pl.program_id(0)
    slots = blocks.shape[1]
    bs = blocks.shape[2]
    bw = mid.shape[0]

    @pl.when(step == 0)
    def _():
        pieces[3 * nbd] = jnp.zeros((2 * bs, 2 * bw), BF16)
        for k, src in enumerate((left, mid, right)):
            for b in range(nbd):
                t = turned(src[:, b * bs : (b + 1) * bs])
                pieces[k * nbd + b, :bs] = t
                pieces[k * nbd + b, bs:] = t
        acc[...] = jnp.zeros_like(acc)
        accw[...] = jnp.zeros_like(accw)

    us, uts = [], []
    for r in range(RB):
        i = step * RB + r
        tot = None
        for s in range(slots):
            both = jnp.concatenate(split(blocks[r, s]), axis=1)
            part = bdot(both, pieces[cols[i * slots + s]])
            tot = part if tot is None else tot + part
        t = tot.T
        u = t[:bw] + t[bw:]
        u_out[:, r * bs : (r + 1) * bs] = u
        us.append(u)
        uts.append(turned(u))
    u = jnp.concatenate(us, axis=1)
    ut = jnp.concatenate(uts, axis=0)
    shi, slo = split(stored[...])
    acc[...] += bdot(shi, ut) + bdot(slo, ut)
    wt = jnp.concatenate([pieces[nbd + step * RB + r, :bs] for r in range(RB)], axis=0)
    both = jnp.concatenate([ut, wt], axis=1)
    start = pl.multiple_of(step * (RB * bs), RB * bs)
    here = pl.ds(start, RB * bs)
    rhi, rlo = split(jnp.concatenate([mid[:, here], prev[:, here], u], axis=0))
    accw[...] += bdot(rhi, both) + bdot(rlo, both)

    @pl.when(step == pl.num_programs(0) - 1)
    def _():
        ks = acc.shape[0]
        t = acc[...].T
        a = t[:bw] + t[bw:]
        m_out[:bw, : ks // 2] = a[:, : ks // 2]
        m_out[bw:, : ks // 2] = a[:, ks // 2 :]
        w = accw[...]
        wu = w[:, :bw] + w[:, bw : 2 * bw]
        ww = w[:bw, 2 * bw : 3 * bw] + w[:bw, 3 * bw :]
        m_out[:bw, ks // 2 :] = jnp.concatenate([wu[:bw], ww], axis=1)
        m_out[bw:, ks // 2 :] = jnp.concatenate([wu[bw : 2 * bw], wu[2 * bw :]], axis=1)


def apply_op(cols, blocks, stored, left, mid, right, prev):
    nbd, slots, bs, _ = blocks.shape
    bw, n = mid.shape
    ks = stored.shape[0]
    whole = pl.BlockSpec((bw, n), lambda i, c: (0, 0))
    return pl.pallas_call(
        functools.partial(apply_kernel, nbd=nbd),
        grid_spec=pltpu.PrefetchScalarGridSpec(
            num_scalar_prefetch=1,
            grid=(nbd // RB,),
            in_specs=[
                pl.BlockSpec((RB, slots, bs, bs), lambda i, c: (i, 0, 0, 0)),
                pl.BlockSpec((ks, RB * bs), lambda i, c: (0, i)),
                whole,
                whole,
                whole,
                whole,
            ],
            out_specs=[
                pl.BlockSpec((bw, RB * bs), lambda i, c: (0, i)),
                pl.BlockSpec((2 * bw, ks // 2 + 2 * bw), lambda i, c: (0, 0)),
            ],
            scratch_shapes=[
                pltpu.VMEM((3 * nbd + 1, 2 * bs, 2 * bw), BF16),
                pltpu.VMEM((ks, 2 * bw), F32),
                pltpu.VMEM((3 * bw, 4 * bw), F32),
            ],
        ),
        out_shape=[
            jax.ShapeDtypeStruct((bw, n), F32),
            jax.ShapeDtypeStruct((2 * bw, ks // 2 + 2 * bw), F32),
        ],
        compiler_params=pltpu.CompilerParams(vmem_limit_bytes=VMEM_LIMIT),
        name="apply_op",
    )(cols, blocks, stored, left, mid, right, prev)


def project_kernel(cs, cw, stored, *refs):
    arrays, out = refs[:-1], refs[-1]
    bw = cs.shape[0]
    chi, clo = split(jnp.concatenate([cs[...], cw[...]], axis=1))
    dhi, dlo = split(jnp.concatenate([stored[...]] + [a[...] for a in arrays], axis=0))
    t = bdot(jnp.concatenate([chi, clo], axis=0), dhi)
    out[...] = t[:bw] + t[bw:] + bdot(chi, dlo)


def project(cs, cw, stored, *arrays):
    ks, n = stored.shape
    bw = cs.shape[0]
    return pl.pallas_call(
        project_kernel,
        grid=(n // TILE,),
        in_specs=[
            pl.BlockSpec(cs.shape, lambda i: (0, 0)),
            pl.BlockSpec(cw.shape, lambda i: (0, 0)),
            pl.BlockSpec((ks, TILE), lambda i: (0, i)),
        ]
        + [pl.BlockSpec((bw, TILE), lambda i: (0, i))] * len(arrays),
        out_specs=pl.BlockSpec((bw, TILE), lambda i: (0, i)),
        out_shape=jax.ShapeDtypeStruct((bw, n), F32),
        compiler_params=pltpu.CompilerParams(vmem_limit_bytes=VMEM_LIMIT),
        name="project",
    )(cs, cw, stored, *arrays)


PANEL = 4


def factor_of(gram):
    n = gram.shape[0]
    row = lax.broadcasted_iota(jnp.int32, (n, 2 * n), 0)
    lane = lax.broadcasted_iota(jnp.int32, (n, 2 * n), 1)
    eye = (lane == row + n).astype(F32)
    m = jnp.where(lane < n, jnp.concatenate([gram, gram], axis=1), eye)
    scale = jnp.zeros((n, 2 * n), F32)
    for p in range(0, n, PANEL):
        cols = [jnp.broadcast_to(m[:, p + j : p + j + 1], (n, 2 * n)) for j in range(PANEL)]
        for j in range(PANEL):
            k = p + j
            pivot = cols[j][k : k + 1]
            root = lax.rsqrt(pivot)
            root = root * (1.5 - 0.5 * pivot * root * root)
            f = jnp.where(row > k, cols[j] * (root * root), 0.0)
            scale = jnp.where(row == k, root, scale)
            m = m - f * m[k : k + 1]
            for q in range(j + 1, PANEL):
                cols[q] = cols[q] - f * cols[q][k : k + 1]
    m = m * scale
    upper = jnp.where(lane >= row, m, 0.0)[:, :n]
    return upper, m[:, n:]


def unpacked(t, bw):
    half = t.shape[1] - 2 * bw
    mst = jnp.concatenate([t[:bw, :half], t[bw:, :half]], axis=1)
    a = t[:bw, half:]
    b = t[bw:, half:]
    return mst, a[:, :bw], a[:, bw:], b[:, :bw], b[:, bw:]


def second_kernel(t, s, c3t, cs, cw, diag, upper, e_out, k_out, c2t_out, c2vt_out):
    bw = c3t.shape[0]
    mst, h, g, _, _ = unpacked(t[...], bw)
    _, e1 = factor_of(g)
    k1t = dot_nn(e1, c3t[...])
    c1t = dot_nn(e1, mst)
    c1vt = dot_nt(e1, dot_nn(e1, h))
    c2t = c1t - dot_nn(c1t, s[...]) - dot_nn(c1vt, k1t)
    c2vt = -dot_nt(c1t, k1t)
    dvt = c1vt + c2vt
    cs[...] = -(c1t + c2t)
    cw[...] = jnp.concatenate([e1, -dot_nn(dvt, e1)], axis=1)
    diag[...] = dvt.T
    upper[...] = jnp.zeros_like(upper)
    e_out[...] = e1
    k_out[...] = k1t
    c2t_out[...] = c2t
    c2vt_out[...] = c2vt


def after_kernel(s, k1t, c2t, c2vt, c3st, c3vt):
    c3st[...] = c2t[...] - dot_nn(c2t[...], s[...]) - dot_nn(c2vt[...], k1t[...])
    c3vt[...] = -dot_nt(c2t[...], k1t[...])


def third_kernel(t, s, c3st, c3vt, k1t_ref, e1_ref, cs, cw, diag, upper2, upper3, *, size):
    bw = c3st.shape[0]
    k1t, e1, sm = k1t_ref[...], e1_ref[...], s[...]
    mst, h, g, h12, uu = unpacked(t[...], bw)
    lt2, e2 = factor_of(g)
    upper2[...] = lt2
    k2t = dot_nn(e2, c3st[...])
    n12t = dot_nn(e2, c3vt[...])
    c1t = dot_nn(e2, mst)
    c1at = dot_nt(e2, dot_nn(e2, h))
    c1bt = dot_nt(e2, dot_nn(e1, h12))
    yy = dot_nt(dot_nn(e2, uu), e2)
    dst = 2.0 * c1t - dot_nn(c1t, sm) - dot_nn(c1at, k2t) - dot_nn(c1bt, k1t)
    dat = c1at - dot_nt(c1t, k2t) - dot_nt(c1bt, n12t)
    dbt = c1bt - dot_nt(c1t, k1t) - dot_nn(c1at, n12t)
    diag[...] = dat.T
    c3s = c1t - dot_nn(dst, sm) - dot_nn(dat, k2t) - dot_nn(dbt, k1t)
    c3a = c1at - dot_nt(dst, k2t) - dat - dot_nt(dbt, n12t)
    c3b = c1bt - dot_nt(dst, k1t) - dot_nn(dat, n12t) - dbt
    g3 = yy - dot_nt(c1t, dst) - dot_nt(dst, c3s)
    g3 = g3 - dot_nt(c1at, dat) - dot_nt(dat, c3a) - dot_nt(c1bt, dbt) - dot_nt(dbt, c3b)
    lt3, e3 = factor_of(0.5 * (g3 + g3.T))
    upper3[...] = lt3
    e3 = e3 * math.sqrt(size)
    cs[...] = -dot_nn(e3, dst)
    cw[...] = jnp.concatenate(
        [dot_nn(e3, e2), -dot_nn(e3, dot_nn(dat, e2)), -dot_nn(e3, dot_nn(dbt, e1))], axis=1
    )


def small(kernel, name, shapes, *args):
    return pl.pallas_call(
        kernel,
        out_shape=[jax.ShapeDtypeStruct(s, F32) for s in shapes],
        compiler_params=pltpu.CompilerParams(vmem_limit_bytes=VMEM_LIMIT),
        name=name,
    )(*args)


def on_device(blocks, pattern, counts, stored, start_block):
    nbd, slots, bs, _ = blocks.shape
    bw, n = start_block.shape
    ks = stored.shape[0]
    half = ks // 2
    devices = lax.axis_size(AXES)
    position = lax.axis_index(AXES)
    nb = nbd * devices
    local = (pattern - (position - 1) * nbd) % nb
    used = jnp.arange(slots, dtype=jnp.int32)[None, :] < counts[:, None]
    cols = jnp.where(used, local, 3 * nbd).reshape(-1)
    up = [(i, (i + 1) % devices) for i in range(devices)]
    down = [(j, i) for i, j in up]

    def halo(w):
        return lax.ppermute(w, AXES, up), lax.ppermute(w, AXES, down)

    top = dot_nt(stored[:half], stored, HIGH)
    corner = dot_nt(stored[half:], stored[half:], HIGH)
    first = dot_nt(stored, start_block, HIGH)
    packed = total(jnp.concatenate([top, corner, first[:half], first[half:]], axis=1))
    s12 = packed[:, half:ks]
    s = jnp.concatenate(
        [packed[:, :ks], jnp.concatenate([s12.T, packed[:, ks : ks + half]], axis=1)], axis=0
    )
    c1 = jnp.concatenate([packed[:, ks + half : ks + half + bw], packed[:, ks + half + bw :]], axis=0)
    c1t = c1.T
    dt = 2.0 * c1t - dot_nn(c1t, s)
    w1 = project(-dt, jnp.eye(bw, dtype=F32), stored, start_block)
    c3t = c1t - dot_nn(dt, s)

    left, right = halo(w1)
    u1, m1 = apply_op(cols, blocks, stored, left, w1, right, w1)
    sq, wide = (bw, bw), (bw, ks)
    cs, cw, diag1, _, e1, k1t, c2t, c2vt = small(
        second_kernel, "second", [wide, (bw, 2 * bw), sq, sq, sq, wide, wide, sq], total(m1), s, c3t
    )
    w2 = project(cs, cw, stored, u1, w1)
    c3st, c3vt = small(after_kernel, "after", [wide, sq], s, k1t, c2t, c2vt)

    left, right = halo(w2)
    u2, m2 = apply_op(cols, blocks, stored, left, w2, right, w1)
    cs, cw, diag2, upper2, upper3 = small(
        functools.partial(third_kernel, size=nb * bs),
        "third",
        [wide, (bw, 3 * bw), sq, sq, sq],
        total(m2), s, c3st, c3vt, k1t, e1,
    )
    last = project(cs, cw, stored, u2, w2, w1)
    return jnp.stack([diag1, diag2]), jnp.stack([upper2, upper3]), last


def solution(mesh):
    in_specs = (
        P(AXES, None, None, None),
        P(AXES, None),
        P(AXES),
        P(None, AXES),
        P(None, AXES),
    )
    out_specs = (P(), P(), P(None, AXES))
    return jax.shard_map(on_device, mesh=mesh, in_specs=in_specs, out_specs=out_specs, check_vma=False)
```

profile of v0, /device:TPU:1, one launch (start us, length us, event | category | flops | bytes accessed | tf_op | source)
XLA Modules:
  0.0 257.3 jit_solution(425580659973599536)
XLA Ops:
  0.6 0.0 slice-start
  0.7 4.5 %fusion = f32[256,256]{1,0:T(8,128)S(1)} fusion(f32[512,3072]{1,0:T(8,128)} %stored.9), kind=kOutput, calls=%fused_computation | convolution fusion | flops 1207959552 | bytes 3407872 | tf_op jit(solution)/shard_map/dot_general | solution.py:22
  5.1 0.0 slice-start.1
  5.2 6.8 %fusion.2 = f32[256,512]{1,0:T(8,128)S(1)} fusion(f32[512,3072]{1,0:T(8,128)} %stored.9), kind=kOutput, calls=%fused_computation.2 | convolution fusion | flops 2415919104 | bytes 9961472 | tf_op jit(solution)/shard_map/dot_general | solution.py:22
  12.0 2.6 %fusion.10 = f32[512,64]{1,0:T(8,128)S(1)} fusion(f32[512,3072]{1,0:T(8,128)S(1)} %bitcast.32, f32[64,3072]{1,0:T(8,128)S(1)} %copy-done), kind=kOutput, calls=%fused_computation.25 | convolution fusion | flops 603979776 | bytes 7208960 | tf_op jit(solution)/shard_map/dot_general | solution.py:22
  14.7 0.1 pad_maximum_fusion
  14.8 0.9 all_to_all.43
  15.7 28.8 %all_to_all.50 = f32[128,1,1792]{2,1,0:T(1,128)S(1)} all-to-all(f32[128,1,1792]{2,1,0:T(1,128)S(1)} %all_to_all.43), channel_id=1, replica_groups=mesh['row'=4,'basis'=8,'rep'=4] {'row','basis','rep'}, dimensions={0} | all-to-all | bytes 1835008 | tf_op jit(solution)/shard_map/all_to_all | solution.py:39
  44.5 0.6 reduce_sum.27
  45.1 1.4 broadcast_in_dim.11
  46.5 4.5 %all-to-all-start.1 = ((f32[128,1,1792]{2,1,0:T(1,128)}), f32[128,1,1792]{2,1,0:T(1,128)S(1)}, u32[]{:S(2)}, u32[]{:S(2)}) async-start(f32[128,1,1792]{2,1,0:T(1,128)} %broadcast_in_dim.11), calls=%async_computation.1 | async-start | bytes 1835008 | tf_op jit(solution)/shard_map/all_to_all | solution.py:41
  51.0 17.5 %all-to-all-done.1 = f32[128,1,1792]{2,1,0:T(1,128)S(1)} async-done(((f32[128,1,1792]{2,1,0:T(1,128)}), f32[128,1,1792]{2,1,0:T(1,128)S(1)}, u32[]{:S(2)}, u32[]{:S(2)}) %all-to-all-start.1) | async-done | bytes 917536 | tf_op jit(solution)/shard_map/all_to_all | solution.py:41
  68.5 2.2 reduce.3
  70.7 0.1 reshape.41
  70.8 0.1 fusion.7
  71.0 0.1 slice.41
  71.0 0.0 copy-start.13
  71.0 0.0 copy-start.19
  71.0 0.0 copy-start.20
  71.1 0.1 copy.42
  71.2 2.5 fusion.9
  73.8 0.1 copy.44.cs
  73.9 4.3 %project.3.mid.prev.refs_1_.refs_2_ = f32[64,3072]{1,0:T(8,128)S(1)} custom-call(f32[64,512]{1,0:T(8,128)S(1)} %copy.44.cs, f32[64,64]{1,0:T(8,128)S(1)} %fusion.4.cw, f32[512,3072]{1,0:T(8,128)} %stored.9, f32[64,3072]{1,0:T(8,128)S(1)} %copy-done), custom_call_target="tpu_custom_call" | custom-call | tf_op jit(solution)/shard_map/project/pallas_call | solution.py:160
  78.3 3.3 %collective-permute-start.1 = (f32[64,3072]{1,0:T(8,128)S(1)}, f32[64,3072]{1,0:T(8,128)S(1)}, u32[]{:S(2)}, u32[]{:S(2)}) collective-permute-start(f32[64,3072]{1,0:T(8,128)S(1)} %project.3.mid.prev.refs_1_.refs_2_), channel_id=1, source_target_pairs={{1,0},{2,1},{3,2},{4,3},{5,4},{6,5},{7,6},{8,7},{9,8},{10,9},{11,1... | collective-permute-start | bytes 2359304 | tf_op jit(solution)/shard_map/ppermute | solution.py:290
  81.6 0.1 copy.37
  81.7 0.1 reshape.40.cols
  81.8 16.7 %collective-permute-done.1.right = f32[64,3072]{1,0:T(8,128)S(1)} collective-permute-done((f32[64,3072]{1,0:T(8,128)S(1)}, f32[64,3072]{1,0:T(8,128)S(1)}, u32[]{:S(2)}, u32[]{:S(2)}) %collective-permute-start.1) | collective-permute-done | bytes 786464 | tf_op jit(solution)/shard_map/ppermute | solution.py:290
  98.5 7.5 %collective-permute-done.left = f32[64,3072]{1,0:T(8,128)S(1)} collective-permute-done((f32[64,3072]{1,0:T(8,128)S(1)}, f32[64,3072]{1,0:T(8,128)S(1)}, u32[]{:S(2)}, u32[]{:S(2)}) %collective-permute-start) | collective-permute-done | bytes 786464 | tf_op jit(solution)/shard_map/ppermute | solution.py:290
  106.0 16.2 %apply_op.2 = (f32[64,3072]{1,0:T(8,128)S(1)}, f32[128,384]{1,0:T(8,128)S(1)}) custom-call(s32[168]{0:T(256)S(1)} %reshape.40.cols, f32[24,7,128,128]{3,2,1,0:T(8,128)} %blocks.3, f32[512,3072]{1,0:T(8,128)} %stored.9, f32[64,3072]{1,0:T(8,128)S(1)} %collective-permute-done.left, f32[64,3072]{1,0:T(8,128)S(1)} %project.3.mid.prev.refs_1_.refs_2_, ...), custom_call_target="tpu_custom_call" | custom-call | tf_op jit(solution)/shard_map/apply_op/pallas_call | solution.py:116
  122.3 0.2 copy.45
  122.5 14.0 %all_to_all.51 = f32[128,1,384]{2,1,0:T(1,128)S(1)} all-to-all(f32[128,1,384]{2,1,0:T(1,128)S(1)} %copy.45), channel_id=1, replica_groups=mesh['row'=4,'basis'=8,'rep'=4] {'row','basis','rep'}, dimensions={0} | all-to-all | bytes 393216 | tf_op jit(solution)/shard_map/all_to_all | solution.py:39
  136.5 0.2 reduce_sum.28
  136.7 0.8 broadcast_in_dim.12
  137.4 3.9 %all-to-all-start.3 = ((f32[128,1,384]{2,1,0:T(1,128)}), f32[128,1,384]{2,1,0:T(1,128)S(1)}, u32[]{:S(2)}, u32[]{:S(2)}) async-start(f32[128,1,384]{2,1,0:T(1,128)} %broadcast_in_dim.12), calls=%async_computation.3 | async-start | bytes 393216 | tf_op jit(solution)/shard_map/all_to_all | solution.py:41
  141.4 3.1 %convolution_subtract_fusion = f32[64,512]{0,1:T(8,128)S(1)} fusion(f32[64,512]{0,1:T(8,128)} %get-tuple-element.46, f32[256,64]{1,0:T(8,128)} %copy-done.18, f32[256,64]{1,0:T(8,128)S(1)} %copy-done.17, f32[256,256]{1,0:T(8,128)} %copy-done.15, f32[256,256]{1,0:T(8,128)} %copy-done.14, f32[256,512]{1,0:T(8,128)} %copy-done.13), kind=kOutput, calls=%fused_computation.4 | convolution fusion | flops 201916416 | bytes 1441792 | tf_op jit(solution)/shard_map/dot_general | solution.py:30
  144.5 0.1 copy.47.c3t
  144.6 1.3 maximum_maximum_fusion.s
  145.9 6.2 %all-to-all-done.3 = f32[128,1,384]{2,1,0:T(1,128)S(1)} async-done(((f32[128,1,384]{2,1,0:T(1,128)}), f32[128,1,384]{2,1,0:T(1,128)S(1)}, u32[]{:S(2)}, u32[]{:S(2)}) %all-to-all-start.3) | async-done | bytes 196640 | tf_op jit(solution)/shard_map/all_to_all | solution.py:41
  152.1 5.0 %second.1 = (f32[64,512]{1,0:T(8,128)S(1)}, f32[64,128]{1,0:T(8,128)S(1)}, f32[64,64]{1,0:T(8,128)S(1)}, f32[64,64]{1,0:T(8,128)}, f32[64,64]{1,0:T(8,128)S(1)},...) custom-call(f32[128,384]{1,0:T(8,128)S(1)} %bitcast.24, ...), custom_call_target="tpu_custom_call" | custom-call | tf_op jit(solution)/shard_map/second/pallas_call | solution.py:267
  157.0 0.6 copy-done.3
  157.7 0.6 copy-done.11
  158.3 4.4 %project.4.mid.refs_1_ = f32[64,3072]{1,0:T(8,128)S(1)} custom-call(f32[64,512]{1,0:T(8,128)S(1)} %get-tuple-element.23.cs, f32[64,128]{1,0:T(8,128)S(1)} %get-tuple-element.24.cw, f32[512,3072]{1,0:T(8,128)} %stored.9, f32[64,3072]{1,0:T(8,128)S(1)} %get-tuple-element.25.refs_0_, f32[64,3072]{1,0:T(8,128)S(1)} %project.3.mid.prev.refs_1_.refs_2_), custom_call_target="tpu_custom_call" | custom-call | tf_op jit(solution)/shard_map/project/pallas_call | solution.py:160
  162.7 2.5 collective-permute-start.3
  165.2 17.3 %collective-permute-done.3.right = f32[64,3072]{1,0:T(8,128)S(1)} collective-permute-done((f32[64,3072]{1,0:T(8,128)S(1)}, f32[64,3072]{1,0:T(8,128)S(1)}, u32[]{:S(2)}, u32[]{:S(2)}) %collective-permute-start.3) | collective-permute-done | bytes 786464 | tf_op jit(solution)/shard_map/ppermute | solution.py:290
  182.6 7.2 %collective-permute-done.2.left = f32[64,3072]{1,0:T(8,128)S(1)} collective-permute-done((f32[64,3072]{1,0:T(8,128)S(1)}, f32[64,3072]{1,0:T(8,128)S(1)}, u32[]{:S(2)}, u32[]{:S(2)}) %collective-permute-start.2) | collective-permute-done | bytes 786464 | tf_op jit(solution)/shard_map/ppermute | solution.py:290
  189.7 16.2 %apply_op.3 = (f32[64,3072]{1,0:T(8,128)S(1)}, f32[128,384]{1,0:T(8,128)S(1)}) custom-call(s32[168]{0:T(256)S(1)} %reshape.40.cols, f32[24,7,128,128]{3,2,1,0:T(8,128)} %blocks.3, f32[512,3072]{1,0:T(8,128)} %stored.9, f32[64,3072]{1,0:T(8,128)S(1)} %collective-permute-done.2.left, f32[64,3072]{1,0:T(8,128)S(1)} %project.4.mid.refs_1_, ...), custom_call_target="tpu_custom_call" | custom-call | tf_op jit(solution)/shard_map/apply_op/pallas_call | solution.py:116
  206.0 0.2 copy.48
  206.2 14.6 %all_to_all.52 = f32[128,1,384]{2,1,0:T(1,128)} all-to-all(f32[128,1,384]{2,1,0:T(1,128)S(1)} %copy.48), channel_id=1, replica_groups=mesh['row'=4,'basis'=8,'rep'=4] {'row','basis','rep'}, dimensions={0} | all-to-all | bytes 393216 | tf_op jit(solution)/shard_map/all_to_all | solution.py:39
  220.8 1.1 reduce_sum.29
  221.9 0.8 broadcast_in_dim.13
  222.7 4.9 %all-to-all-start.5 = ((f32[128,1,384]{2,1,0:T(1,128)}), f32[128,1,384]{2,1,0:T(1,128)}, u32[]{:S(2)}, u32[]{:S(2)}) async-start(f32[128,1,384]{2,1,0:T(1,128)} %broadcast_in_dim.13), calls=%async_computation.5 | async-start | bytes 393216 | tf_op jit(solution)/shard_map/all_to_all | solution.py:41
  227.6 0.9 copy-done.4
  228.5 0.8 copy-done.12
  229.3 0.9 after.1
  230.1 0.6 copy-done.1
  230.8 0.6 copy-done.7
  231.4 6.6 %all-to-all-done.5 = f32[128,1,384]{2,1,0:T(1,128)} async-done(((f32[128,1,384]{2,1,0:T(1,128)}), f32[128,1,384]{2,1,0:T(1,128)}, u32[]{:S(2)}, u32[]{:S(2)}) %all-to-all-start.5) | async-done | bytes 196640 | tf_op jit(solution)/shard_map/all_to_all | solution.py:41
  238.0 0.9 copy.57
  239.0 0.9 copy-done.2
  239.9 0.8 copy-done.6
  240.6 0.8 copy-done.8
  241.4 10.0 %third.1 = (f32[64,512]{1,0:T(8,128)S(1)}, f32[64,192]{1,0:T(8,128)S(1)}, f32[64,64]{1,0:T(8,128)S(1)}, f32[64,64]{1,0:T(8,128)S(1)}, f32[64,64]{1,0:T(8,128)S(1)}) custom-call(f32[128,384]{1,0:T(8,128)S(1)} %bitcast.23, f32[512,512]{1,0:T(8,128)S(1)} %maximum_maximum_fusion.s, f32[64,512]{1,0:T(8,128)S(1)} %copy-done.2, f32[64,64]{1,0:T(8,128)S(1)} %copy-done.8, ...), custom_call_target="tpu_custom_call" | custom-call | tf_op jit(solution)/shard_map/third/pallas_call | solution.py:267
  251.4 5.3 %project.5 = f32[64,3072]{1,0:T(8,128)} custom-call(f32[64,512]{1,0:T(8,128)S(1)} %get-tuple-element.36.cs, f32[64,192]{1,0:T(8,128)S(1)} %get-tuple-element.37.cw, f32[512,3072]{1,0:T(8,128)} %stored.9, f32[64,3072]{1,0:T(8,128)S(1)} %get-tuple-element.38.refs_0_, f32[64,3072]{1,0:T(8,128)S(1)} %project.4.mid.refs_1_, ...), custom_call_target="tpu_custom_call" | custom-call | tf_op jit(solution)/shard_map/project/pallas_call | solution.py:160
  256.7 0.7 pad_maximum_fusion.3
  (40 shorter events, 0.2 us)
Async XLA Ops:
  0.6 11.4 %slice-start = ((s8[6291456]{0:T(1024)(128)(4,1)}), s8[4194304]{0:T(1024)(128)(4,1)S(1)}, s32[]{:S(2)}) async-start(s8[6291456]{0:T(1024)(128)(4,1)} %bitcast.31), calls=%async_computation.6 | async-start | bytes 8388608
  0.6 11.4 %copy-start = (f32[64,3072]{1,0:T(8,128)S(1)}, f32[64,3072]{1,0:T(8,128)}, u32[]{:S(2)}) copy-start(f32[64,3072]{1,0:T(8,128)} %refs_0_.1) | copy-start | bytes 2359300
  5.1 6.9 %slice-start.1 = ((s8[6291456]{0:T(1024)(128)(4,1)}), s8[2097152]{0:T(1024)(128)(4,1)S(1)}, s32[]{:S(2)}) async-start(s8[6291456]{0:T(1024)(128)(4,1)} %bitcast.31), calls=%async_computation.7 | async-start | bytes 4194304
  46.5 22.0 %all-to-all-start.1 = ((f32[128,1,1792]{2,1,0:T(1,128)}), f32[128,1,1792]{2,1,0:T(1,128)S(1)}, u32[]{:S(2)}, u32[]{:S(2)}) async-start(f32[128,1,1792]{2,1,0:T(1,128)} %broadcast_in_dim.11), calls=%async_computation.1 | async-start | bytes 1835008 | tf_op jit(solution)/shard_map/all_to_all | solution.py:41
  70.9 7.3 %copy-start.16 = (f32[256,64]{1,0:T(8,128)}, f32[256,64]{1,0:T(8,128)S(1)}, u32[]{:S(2)}) copy-start(f32[256,64]{1,0:T(8,128)S(1)} %get-tuple-element.41) | copy-start | bytes 196612
  70.9 27.5 %copy-start.18 = (f32[256,64]{1,0:T(8,128)}, f32[256,64]{1,0:T(8,128)S(1)}, u32[]{:S(2)}) copy-start(f32[256,64]{1,0:T(8,128)S(1)} %get-tuple-element.42) | copy-start | bytes 196612
  71.0 2.8 %copy-start.13 = (f32[256,512]{1,0:T(8,128)}, f32[256,512]{1,0:T(8,128)S(1)}, u32[]{:S(2)}) copy-start(f32[256,512]{1,0:T(8,128)S(1)} %slice.41) | copy-start | bytes 1572868
  71.0 10.5 %copy-start.19 = (s32[24,7]{0,1:T(8,128)S(1)}, s32[24,7]{0,1:T(8,128)}, u32[]{:S(2)}) copy-start(s32[24,7]{0,1:T(8,128)} %param.6) | copy-start | bytes 2020
  71.0 10.5 %copy-start.20 = (s32[24]{0:T(128)S(1)}, s32[24]{0:T(128)}, u32[]{:S(2)}) copy-start(s32[24]{0:T(128)} %param.7) | copy-start | bytes 292
  71.1 10.5 %copy-start.15 = (f32[256,256]{1,0:T(8,128)}, f32[256,256]{1,0:T(8,128)S(1)}, u32[]{:S(2)}) copy-start(f32[256,256]{1,0:T(8,128)S(1)} %get-tuple-element.40) | copy-start | bytes 786436
  71.2 2.5 copy-start.14
  78.3 20.2 %collective-permute-start.1 = (f32[64,3072]{1,0:T(8,128)S(1)}, f32[64,3072]{1,0:T(8,128)S(1)}, u32[]{:S(2)}, u32[]{:S(2)}) collective-permute-start(f32[64,3072]{1,0:T(8,128)S(1)} %project.3.mid.prev.refs_1_.refs_2_), channel_id=1, source_target_pairs={{1,0},{2,1},{3,2},{4,3},{5,4},{6,5},{7,6},{8,7},{9,8},{10,9},{11,1... | collective-permute-start | bytes 2359304 | tf_op jit(solution)/shard_map/ppermute | solution.py:290
  81.5 24.5 %collective-permute-start = (f32[64,3072]{1,0:T(8,128)S(1)}, f32[64,3072]{1,0:T(8,128)S(1)}, u32[]{:S(2)}, u32[]{:S(2)}) collective-permute-start(f32[64,3072]{1,0:T(8,128)S(1)} %project.3.mid.prev.refs_1_.refs_2_), channel_id=1, source_target_pairs={{0,1},{1,2},{2,3},{3,4},{4,5},{5,6},{6,7},{7,8},{8,9},{9,10},{10,1... | collective-permute-start | bytes 2359304 | tf_op jit(solution)/shard_map/ppermute | solution.py:290
  81.8 59.6 %copy-start.17 = (f32[256,64]{1,0:T(8,128)S(1)}, f32[256,64]{1,0:T(8,128)}, u32[]{:S(2)}) copy-start(f32[256,64]{1,0:T(8,128)} %copy-done.16) | copy-start | bytes 196612
  137.4 14.6 %all-to-all-start.3 = ((f32[128,1,384]{2,1,0:T(1,128)}), f32[128,1,384]{2,1,0:T(1,128)S(1)}, u32[]{:S(2)}, u32[]{:S(2)}) async-start(f32[128,1,384]{2,1,0:T(1,128)} %broadcast_in_dim.12), calls=%async_computation.3 | async-start | bytes 393216 | tf_op jit(solution)/shard_map/all_to_all | solution.py:41
  157.0 0.6 copy-start.3
  157.7 0.6 copy-start.11
  158.3 24.3 %copy-start.5 = (f32[64,64]{1,0:T(8,128)}, f32[64,64]{1,0:T(8,128)S(1)}, u32[]{:S(2)}) copy-start(f32[64,64]{1,0:T(8,128)S(1)} %get-tuple-element.32.e1_ref) | copy-start | bytes 49156
  158.3 47.7 %copy-start.9 = (f32[64,64]{1,0:T(8,128)}, f32[64,64]{1,0:T(8,128)S(1)}, u32[]{:S(2)}) copy-start(f32[64,64]{1,0:T(8,128)S(1)} %get-tuple-element.22) | copy-start | bytes 49156
  162.7 19.8 %collective-permute-start.3 = (f32[64,3072]{1,0:T(8,128)S(1)}, f32[64,3072]{1,0:T(8,128)S(1)}, u32[]{:S(2)}, u32[]{:S(2)}) collective-permute-start(f32[64,3072]{1,0:T(8,128)S(1)} %project.4.mid.refs_1_), channel_id=1, source_target_pairs={{1,0},{2,1},{3,2},{4,3},{5,4},{6,5},{7,6},{8,7},{9,8},{10,9},{11,1... | collective-permute-start | bytes 2359304 | tf_op jit(solution)/shard_map/ppermute | solution.py:290
  165.2 24.5 %collective-permute-start.2 = (f32[64,3072]{1,0:T(8,128)S(1)}, f32[64,3072]{1,0:T(8,128)S(1)}, u32[]{:S(2)}, u32[]{:S(2)}) collective-permute-start(f32[64,3072]{1,0:T(8,128)S(1)} %project.4.mid.refs_1_), channel_id=1, source_target_pairs={{0,1},{1,2},{2,3},{3,4},{4,5},{5,6},{6,7},{7,8},{8,9},{9,10},{10,1... | collective-permute-start | bytes 2359304 | tf_op jit(solution)/shard_map/ppermute | solution.py:290
  222.7 15.3 %all-to-all-start.5 = ((f32[128,1,384]{2,1,0:T(1,128)}), f32[128,1,384]{2,1,0:T(1,128)}, u32[]{:S(2)}, u32[]{:S(2)}) async-start(f32[128,1,384]{2,1,0:T(1,128)} %broadcast_in_dim.13), calls=%async_computation.5 | async-start | bytes 393216 | tf_op jit(solution)/shard_map/all_to_all | solution.py:41
  227.6 0.9 copy-start.4
  228.5 0.8 copy-start.12
  230.1 0.6 copy-start.1
  230.8 0.6 copy-start.7
  238.0 18.7 %copy-start.10 = (f32[64,64]{1,0:T(8,128)S(1)}, f32[64,64]{1,0:T(8,128)}, u32[]{:S(2)}) copy-start(f32[64,64]{1,0:T(8,128)} %copy-done.9) | copy-start | bytes 49156
  239.0 0.9 copy-start.2
  239.9 0.8 copy-start.6
  240.6 0.8 copy-start.8
where the time goes:
time: 259 us; the launch traced here: 257 us
  waiting for transfers between devices  79 us (31%)
  Pallas kernels  62.3 us (24%)
  blocking collectives  57.5 us (22%)
  matrix products  19.6 us (8%)
  starting transfers between devices  19.1 us (7%)
  local copies, waits for them, and re-layouts  12.7 us (5%)
  other arithmetic  6.1 us (2%)
    all_to_all x3, blocking collectives, total(): parts = lax.all_to_all(x.reshape(n, x.size // n), AXES, 0, 0, tiled=True)  57.5 us
    ppermute x4, waiting for transfers between devices, halo(): return (lax.ppermute(w, AXES, up), lax.ppermute(w, AXES, down))  48.7 us
    pallas_call x2, Pallas kernels, apply_op(): pl.pallas_call(functools.partial(apply_kernel, nbd=nbd), grid_spec=pltpu....  32.5 us
    all_to_all x3, waiting for transfers between devices, total(): lax.all_to_all(jnp.broadcast_to(mine[None], parts.shape), AXES, 0, 0, til...  30.3 us
    pallas_call x3, Pallas kernels, small(): pl.pallas_call(kernel, out_shape=[jax.ShapeDtypeStruct(s, F32) for s in s...  15.8 us
    pallas_call x3, Pallas kernels, project(): pl.pallas_call(project_kernel, grid=(n // TILE,), in_specs=[pl.BlockSpec(...  14 us
    dot_general x3, matrix products, dot_nt(): lax.dot_general(a, b, (((1,), (1,)), ((), ())), precision=precision, pref...  13.9 us
    all_to_all x3, starting transfers between devices, total(): lax.all_to_all(jnp.broadcast_to(mine[None], parts.shape), AXES, 0, 0, til...  13.3 us
  transfers between devices with their start and end apart: 7, of which 7 were waited for; matrix products, arithmetic and copies ran while one was open for 2% of the time, Pallas kernels for 0%

commit v1 on v0

v1 whole, which is shorter than its diff:
```python
import functools
import math

import jax
import jax.numpy as jnp
from jax import lax
from jax.experimental import pallas as pl
from jax.experimental.pallas import tpu as pltpu
from jax.sharding import PartitionSpec as P

AXES = ("row", "basis", "rep")
HIGH = lax.Precision.HIGH
FULL = lax.Precision.HIGHEST
F32 = jnp.float32
BF16 = jnp.bfloat16
RB = 4
CHUNK = 4
TILE = 512
VMEM_LIMIT = 12 * 1024 * 1024


def dot_nt(a, b, precision=FULL):
    return lax.dot_general(a, b, (((1,), (1,)), ((), ())), precision=precision, preferred_element_type=F32)


def dot_tn(a, b, precision=FULL):
    return lax.dot_general(a, b, (((0,), (0,)), ((), ())), precision=precision, preferred_element_type=F32)


def dot_nn(a, b, precision=FULL):
    return lax.dot_general(a, b, (((1,), (0,)), ((), ())), precision=precision, preferred_element_type=F32)


def bdot(a, b):
    return jnp.dot(a, b, preferred_element_type=F32)


def total(x):
    n = lax.axis_size(AXES)
    parts = lax.all_to_all(x.reshape(n, x.size // n), AXES, 0, 0, tiled=True)
    mine = jnp.sum(parts, axis=0)
    out = lax.all_to_all(jnp.broadcast_to(mine[None], parts.shape), AXES, 0, 0, tiled=True)
    return out.reshape(x.shape)


def split(x):
    hi = x.astype(BF16)
    lo = (x - hi.astype(F32)).astype(BF16)
    return hi, lo


def turned(x):
    hi = x.astype(BF16).astype(F32)
    return jnp.concatenate([hi, x - hi], axis=0).T.astype(BF16)


def add_slots(plan, first, chunks, size, blocks, pieces, tot):
    @pl.loop(0, chunks)
    def _(c):
        parts = []
        for e in range(CHUNK):
            at = first + c * CHUNK + e
            parts.append((plan[at + size], bdot(blocks[plan[at]], pieces[plan[at + 2 * size]])))
        for row, part in parts:
            tot[row] += part


def put_piece(pieces, at, x):
    bs = x.shape[1]
    t = turned(x)
    pieces[at, :bs] = t
    pieces[at, bs:] = t


def near_kernel(plan, blocks, mid, tot, halves, gram, pieces):
    nbd, bs, _ = tot.shape
    bw = mid.shape[0]
    size = plan.shape[0] // 6
    pieces[nbd] = jnp.zeros((2 * bs, 2 * bw), BF16)
    tot[...] = jnp.zeros_like(tot)

    @pl.loop(0, nbd, unroll=4)
    def _(b):
        put_piece(pieces, b, mid[:, pl.ds(pl.multiple_of(b * bs, bs), bs)])

    @pl.loop(0, blocks.shape[0], unroll=4)
    def _(k):
        halves[k] = jnp.concatenate(split(blocks[k]), axis=1)

    add_slots(plan, 1, plan[0], size, halves, pieces, tot)
    g = jnp.zeros((bw, 2 * bw), F32)
    for b in range(0, nbd, RB):
        hi, lo = split(mid[:, b * bs : (b + RB) * bs])
        w = jnp.concatenate([pieces[b + r, :bs] for r in range(RB)], axis=0)
        g = g + bdot(hi, w) + bdot(lo, w)
    gram[...] = g[:, :bw] + g[:, bw:]


def far_kernel(plan, halves, stored, left, right, near, mid, prev, gram, u_out, m_out, tot, pieces, ut, acc, accw):
    nbd, bs, _ = tot.shape
    bw, n = mid.shape
    ks = stored.shape[0]
    size = plan.shape[0] // 6
    pieces[2 * nbd] = jnp.zeros((2 * bs, 2 * bw), BF16)
    for k, src in enumerate((left, right)):

        @pl.loop(0, nbd, unroll=4)
        def _(b):
            put_piece(pieces, k * nbd + b, src[:, pl.ds(pl.multiple_of(b * bs, bs), bs)])

    tot[...] = jnp.zeros_like(tot)
    add_slots(plan, 3 * size + 1, plan[3 * size], size, halves, pieces, tot)

    @pl.loop(0, nbd, unroll=RB)
    def _(b):
        here = pl.ds(pl.multiple_of(b * bs, bs), bs)
        t = (tot[b] + near[b]).T
        u = t[:bw] + t[bw:]
        u_out[:, here] = u
        ut[here] = turned(u)

    acc[...] = jnp.zeros_like(acc)
    accw[...] = jnp.zeros_like(accw)

    @pl.loop(0, n // TILE)
    def _(b):
        here = pl.ds(pl.multiple_of(b * TILE, TILE), TILE)
        t = ut[here]
        shi, slo = split(stored[:, here])
        acc[...] += bdot(shi, t) + bdot(slo, t)
        rhi, rlo = split(jnp.concatenate([mid[:, here], prev[:, here], u_out[:, here]], axis=0))
        accw[...] += bdot(rhi, t) + bdot(rlo, t)

    t = acc[...].T
    a = t[:bw] + t[bw:]
    m_out[:bw, : ks // 2] = a[:, : ks // 2]
    m_out[bw:, : ks // 2] = a[:, ks // 2 :]
    w = accw[...]
    w = w[:, :bw] + w[:, bw:]
    m_out[:bw, ks // 2 :] = jnp.concatenate([w[:bw], gram[...]], axis=1)
    m_out[bw:, ks // 2 :] = jnp.concatenate([w[bw : 2 * bw], w[2 * bw :]], axis=1)


VMEM = pl.BlockSpec(memory_space=pltpu.VMEM)
SMEM = pl.BlockSpec(memory_space=pltpu.SMEM)


def near_op(plan, blocks, mid, nbd):
    _, bs, _ = blocks.shape
    bw, n = mid.shape
    return pl.pallas_call(
        near_kernel,
        in_specs=[SMEM, VMEM, VMEM],
        out_specs=[VMEM] * 3,
        out_shape=[
            jax.ShapeDtypeStruct((nbd, bs, 2 * bw), F32),
            jax.ShapeDtypeStruct((blocks.shape[0], bs, 2 * bs), BF16),
            jax.ShapeDtypeStruct((bw, bw), F32),
        ],
        scratch_shapes=[pltpu.VMEM((nbd + 1, 2 * bs, 2 * bw), BF16)],
        compiler_params=pltpu.CompilerParams(vmem_limit_bytes=VMEM_LIMIT),
        cost_estimate=pl.CostEstimate(flops=2 * 10**9, bytes_accessed=12 * 2**20, transcendentals=0),
        name="near_op",
    )(plan, blocks, mid)


def far_op(plan, halves, stored, left, right, near, mid, prev, gram):
    nbd, bs, _ = near.shape
    bw, n = mid.shape
    ks = stored.shape[0]
    return pl.pallas_call(
        far_kernel,
        in_specs=[SMEM] + [VMEM] * 8,
        out_specs=[VMEM] * 2,
        scratch_shapes=[
            pltpu.VMEM((nbd, bs, 2 * bw), F32),
            pltpu.VMEM((2 * nbd + 1, 2 * bs, 2 * bw), BF16),
            pltpu.VMEM((n, 2 * bw), BF16),
            pltpu.VMEM((ks, 2 * bw), F32),
            pltpu.VMEM((3 * bw, 2 * bw), F32),
        ],
        out_shape=[
            jax.ShapeDtypeStruct((bw, n), F32),
            jax.ShapeDtypeStruct((2 * bw, ks // 2 + 2 * bw), F32),
        ],
        compiler_params=pltpu.CompilerParams(vmem_limit_bytes=VMEM_LIMIT),
        cost_estimate=pl.CostEstimate(flops=2 * 10**9, bytes_accessed=20 * 2**20, transcendentals=0),
        name="far_op",
    )(plan, halves, stored, left, right, near, mid, prev, gram)


def make_plan(local, used, nbd):
    slots = local.shape[1]
    total_slots = nbd * slots
    size = -(-total_slots // CHUNK) * CHUNK + 1
    local, used = local.reshape(-1), used.reshape(-1)
    mine = (local >= nbd) & (local < 2 * nbd)
    ids = jnp.arange(total_slots, dtype=jnp.int32)
    rows = jnp.arange(size - 1, dtype=jnp.int32)
    out = []
    for flag, piece, empty in (
        (used & mine, local - nbd, nbd),
        (used & ~mine, jnp.where(local < nbd, local, local - nbd), 2 * nbd),
    ):
        before = jnp.sum(((ids[None, :] < ids[:, None]) & flag[None, :]).astype(jnp.int32), axis=1)
        hit = (before[None, :] == rows[:, None]) & flag[None, :]
        count = jnp.sum(flag.astype(jnp.int32))
        slot = jnp.sum(jnp.where(hit, ids[None, :], 0), axis=1)
        where = jnp.sum(jnp.where(hit, piece[None, :], 0), axis=1)
        where = jnp.where(rows < count, where, empty)
        zero = jnp.zeros((1,), jnp.int32)
        chunks = (count + CHUNK - 1) // CHUNK
        out += [chunks[None], slot, zero, slot // slots, zero, where]
    return jnp.concatenate(out)


def project_kernel(cs, cw, stored, *refs):
    arrays, out = refs[:-1], refs[-1]
    bw, n = out.shape
    chi, clo = split(jnp.concatenate([cs[...], cw[...]], axis=1))
    c2 = jnp.concatenate([chi, clo], axis=0)

    @pl.loop(0, n // TILE)
    def _(i):
        here = pl.ds(pl.multiple_of(i * TILE, TILE), TILE)
        dhi, dlo = split(jnp.concatenate([stored[:, here]] + [a[:, here] for a in arrays], axis=0))
        t = bdot(c2, dhi)
        out[:, here] = t[:bw] + t[bw:] + bdot(chi, dlo)


def project(cs, cw, stored, *arrays):
    vmem = pl.BlockSpec(memory_space=pltpu.VMEM)
    return pl.pallas_call(
        project_kernel,
        in_specs=[vmem] * (3 + len(arrays)),
        out_specs=vmem,
        out_shape=jax.ShapeDtypeStruct(arrays[0].shape, F32),
        compiler_params=pltpu.CompilerParams(vmem_limit_bytes=VMEM_LIMIT),
        name="project",
    )(cs, cw, stored, *arrays)


PANEL = 4


def factor_of(gram):
    n = gram.shape[0]
    row = lax.broadcasted_iota(jnp.int32, (n, 2 * n), 0)
    lane = lax.broadcasted_iota(jnp.int32, (n, 2 * n), 1)
    eye = (lane == row + n).astype(F32)
    m = jnp.where(lane < n, jnp.concatenate([gram, gram], axis=1), eye)
    scale = jnp.zeros((n, 2 * n), F32)
    for p in range(0, n, PANEL):
        cols = [jnp.broadcast_to(m[:, p + j : p + j + 1], (n, 2 * n)) for j in range(PANEL)]
        for j in range(PANEL):
            k = p + j
            pivot = cols[j][k : k + 1]
            root = lax.rsqrt(pivot)
            root = root * (1.5 - 0.5 * pivot * root * root)
            f = jnp.where(row > k, cols[j] * (root * root), 0.0)
            scale = jnp.where(row == k, root, scale)
            m = m - f * m[k : k + 1]
            for q in range(j + 1, PANEL):
                cols[q] = cols[q] - f * cols[q][k : k + 1]
    m = m * scale
    upper = jnp.where(lane >= row, m, 0.0)[:, :n]
    return upper, m[:, n:]


def unpacked(t, bw):
    half = t.shape[1] - 2 * bw
    mst = jnp.concatenate([t[:bw, :half], t[bw:, :half]], axis=1)
    a = t[:bw, half:]
    b = t[bw:, half:]
    return mst, a[:, :bw], a[:, bw:], b[:, :bw], b[:, bw:]


def first_kernel(packed, s, c1t_out, minus_dt):
    half = packed.shape[0]
    bw = c1t_out.shape[0]
    s12 = packed[:, half : 2 * half]
    s[:half] = packed[:, : 2 * half]
    s[half:] = jnp.concatenate([s12.T, packed[:, 2 * half : 3 * half]], axis=1)
    t = packed[:, 3 * half :].T
    c1t = jnp.concatenate([t[:bw], t[bw:]], axis=1)
    c1t_out[...] = c1t
    minus_dt[...] = dot_nn(c1t, s[...]) - 2.0 * c1t


def after_first_kernel(s, c1t, minus_dt, c3t):
    c3t[...] = c1t[...] + dot_nn(minus_dt[...], s[...])


def second_kernel(t, s, c3t, cs, cw, keep):
    bw = c3t.shape[0]
    mst, h, g, _, _ = unpacked(t[...], bw)
    _, e1 = factor_of(g)
    k1t = dot_nn(e1, c3t[...])
    c1t = dot_nn(e1, mst)
    c1vt = dot_nt(e1, dot_nn(e1, h))
    c2t = c1t - dot_nn(c1t, s[...]) - dot_nn(c1vt, k1t)
    c2vt = -dot_nt(c1t, k1t)
    dvt = c1vt + c2vt
    cs[...] = -(c1t + c2t)
    cw[...] = jnp.concatenate([e1, -dot_nn(dvt, e1)], axis=1)
    keep[:bw] = k1t
    keep[bw : 2 * bw] = c2t
    keep[2 * bw :, : 4 * bw] = jnp.concatenate([e1, c2vt, dvt.T, dvt], axis=1)


def after_kernel(s, keep, c3):
    bw = c3.shape[0]
    k1t, c2t, c2vt = keep[:bw], keep[bw : 2 * bw], keep[2 * bw :, bw : 2 * bw]
    c3[:, : s.shape[0]] = c2t - dot_nn(c2t, s[...]) - dot_nn(c2vt, k1t)
    c3vt = -dot_nt(c2t, k1t)
    c3[:, s.shape[0] :] = jnp.concatenate([c3vt, c3vt], axis=1)


def third_kernel(t, s, c3, keep, cs, cw, diags, uppers, *, size):
    bw = c3.shape[0]
    sm = s[...]
    k1t, e1 = keep[:bw], keep[2 * bw :, :bw]
    c3st, c3vt = c3[:, : sm.shape[0]], c3[:, sm.shape[0] : sm.shape[0] + bw]
    mst, h, g, h12, uu = unpacked(t[...], bw)
    lt2, e2 = factor_of(g)
    uppers[0] = lt2
    k2t = dot_nn(e2, c3st)
    n12t = dot_nn(e2, c3vt)
    c1t = dot_nn(e2, mst)
    c1at = dot_nt(e2, dot_nn(e2, h))
    c1bt = dot_nt(e2, dot_nn(e1, h12))
    yy = dot_nt(dot_nn(e2, uu), e2)
    dst = 2.0 * c1t - dot_nn(c1t, sm) - dot_nn(c1at, k2t) - dot_nn(c1bt, k1t)
    dat = c1at - dot_nt(c1t, k2t) - dot_nt(c1bt, n12t)
    dbt = c1bt - dot_nt(c1t, k1t) - dot_nn(c1at, n12t)
    diags[0] = keep[2 * bw :, 2 * bw : 3 * bw]
    diags[1] = dat.T
    c3s = c1t - dot_nn(dst, sm) - dot_nn(dat, k2t) - dot_nn(dbt, k1t)
    c3a = c1at - dot_nt(dst, k2t) - dat - dot_nt(dbt, n12t)
    c3b = c1bt - dot_nt(dst, k1t) - dot_nn(dat, n12t) - dbt
    g3 = yy - dot_nt(c1t, dst) - dot_nt(dst, c3s)
    g3 = g3 - dot_nt(c1at, dat) - dot_nt(dat, c3a) - dot_nt(c1bt, dbt) - dot_nt(dbt, c3b)
    lt3, e3 = factor_of(0.5 * (g3 + g3.T))
    uppers[1] = lt3
    e3 = e3 * math.sqrt(size)
    cs[...] = -dot_nn(e3, dst)
    cw[...] = jnp.concatenate(
        [dot_nn(e3, e2), -dot_nn(e3, dot_nn(dat, e2)), -dot_nn(e3, dot_nn(dbt, e1))], axis=1
    )


def small(kernel, name, shapes, *args, flops=10**10):
    return pl.pallas_call(
        kernel,
        out_shape=[jax.ShapeDtypeStruct(s, F32) for s in shapes],
        compiler_params=pltpu.CompilerParams(vmem_limit_bytes=VMEM_LIMIT),
        cost_estimate=pl.CostEstimate(flops=flops, bytes_accessed=2 * 2**20, transcendentals=0),
        name=name,
    )(*args)


def on_device(blocks, pattern, counts, stored, start_block):
    nbd, slots, bs, _ = blocks.shape
    bw, n = start_block.shape
    ks = stored.shape[0]
    half = ks // 2
    devices = lax.axis_size(AXES)
    position = lax.axis_index(AXES)
    nb = nbd * devices
    local = (pattern - (position - 1) * nbd) % nb
    used = jnp.arange(slots, dtype=jnp.int32)[None, :] < counts[:, None]
    plan = make_plan(local, used, nbd)
    tiles = blocks.reshape(nbd * slots, bs, bs)
    up = [(i, (i + 1) % devices) for i in range(devices)]
    down = [(j, i) for i, j in up]

    def halo(w):
        return lax.ppermute(w, AXES, up), lax.ppermute(w, AXES, down)

    top = dot_nt(stored[:half], stored, HIGH)
    corner = dot_nt(stored[half:], stored[half:], HIGH)
    first = dot_nt(stored, start_block, HIGH)
    packed = total(jnp.concatenate([top, corner, first[:half], first[half:]], axis=1))
    wide = (bw, ks)
    s, c1t, minus_dt = small(first_kernel, "first", [(ks, ks), wide, wide], packed)
    w1 = project(minus_dt, jnp.eye(bw, dtype=F32), stored, start_block)
    (c3t,) = small(after_first_kernel, "after_first", [wide], s, c1t, minus_dt, flops=10**8)

    def apply(w, prev):
        left, right = halo(w)
        near, halves, gram = near_op(plan, tiles, w, nbd)
        return far_op(plan, halves, stored, left, right, near, w, prev, gram)

    u1, m1 = apply(w1, w1)
    cs, cw, keep = small(second_kernel, "second", [wide, (bw, 2 * bw), (3 * bw, ks)], total(m1), s, c3t)
    w2 = project(cs, cw, stored, u1, w1)
    (c3,) = small(after_kernel, "after", [(bw, ks + 2 * bw)], s, keep, flops=10**8)

    u2, m2 = apply(w2, w1)
    cs, cw, diags, uppers = small(
        functools.partial(third_kernel, size=nb * bs),
        "third",
        [wide, (bw, 3 * bw), (2, bw, bw), (2, bw, bw)],
        total(m2), s, c3, keep,
    )
    return diags, uppers, project(cs, cw, stored, u2, w2, w1)


def solution(mesh):
    in_specs = (
        P(AXES, None, None, None),
        P(AXES, None),
        P(AXES),
        P(None, AXES),
        P(None, AXES),
    )
    out_specs = (P(), P(), P(None, AXES))
    return jax.shard_map(on_device, mesh=mesh, in_specs=in_specs, out_specs=out_specs, check_vma=False)
```

time: 259 us -> 250 us (0.965); the launches traced: 257 us -> 253 us
  starting transfers between devices: 19.1 us -> 40.9 us
  blocking collectives: 57.5 us -> 39.6 us
  waiting for transfers between devices: 79 us -> 65.9 us
  local copies, waits for them, and re-layouts: 12.7 us -> 22 us
  matrix products: 19.6 us -> 11.1 us
    ppermute x4, waiting for transfers between devices: 48.7 us -> 15 us  [halo(): return (lax.ppermute(w, AXES, up), lax.ppermute(w, AXES, down))]
    all_to_all x3 -> x2, blocking collectives: 57.5 us -> 39.6 us  [total(): parts = lax.all_to_all(x.reshape(n, x.size // n), AXES, 0, 0, tiled=True)]
    all_to_all x0 -> x1, waiting for transfers between devices: none -> 17.1 us  [total(): parts = lax.all_to_all(x.reshape(n, x.size // n), AXES, 0, 0, tiled=True)]
    all_to_all x0 -> x1, starting transfers between devices: none -> 11.5 us  [total(): parts = lax.all_to_all(x.reshape(n, x.size // n), AXES, 0, 0, tiled=True)]
    ppermute x4, starting transfers between devices: 5.82 us -> 15.1 us  [halo(): return (lax.ppermute(w, AXES, up), lax.ppermute(w, AXES, down))]
    unnamed x48 -> x58, local copies, waits for them, and re-layouts: 7.6 us -> 14.8 us
    dot_general x2 -> x0, matrix products: 5.64 us -> none  [dot_nn(): lax.dot_general(a, b, (((1,), (0,)), ((), ())), precision=precision, pref...]
    all_to_all x3, waiting for transfers between devices: 30.3 us -> 33.7 us  [total(): lax.all_to_all(jnp.broadcast_to(mine[None], parts.shape), AXES, 0, 0, til...]
  transfers between devices with their start and end apart: 7 -> 8, of which waited for: 7 -> 6; matrix products, arithmetic and copies ran while one was open for 2% -> 1% of each run, Pallas kernels for 0% -> 5%
where the time goes in v1:
time: 250 us; the launch traced here: 253 us
  waiting for transfers between devices  65.9 us (26%)
  Pallas kernels  63.7 us (25%)
  starting transfers between devices  40.9 us (16%)
  blocking collectives  39.6 us (16%)
  local copies, waits for them, and re-layouts  22 us (9%)
  matrix products  11.1 us (4%)
  other arithmetic  6.89 us (3%)
    all_to_all x2, blocking collectives, total(): parts = lax.all_to_all(x.reshape(n, x.size // n), AXES, 0, 0, tiled=True)  39.6 us
    all_to_all x3, waiting for transfers between devices, total(): lax.all_to_all(jnp.broadcast_to(mine[None], parts.shape), AXES, 0, 0, til...  33.7 us
    pallas_call x2, Pallas kernels, far_op(): pl.pallas_call(far_kernel, in_specs=[SMEM] + [VMEM] * 8, out_specs=[VMEM]...  26.4 us
    pallas_call x5, Pallas kernels, small(): pl.pallas_call(kernel, out_shape=[jax.ShapeDtypeStruct(s, F32) for s in s...  17.5 us
    all_to_all x1, waiting for transfers between devices, total(): parts = lax.all_to_all(x.reshape(n, x.size // n), AXES, 0, 0, tiled=True)  17.1 us
    ppermute x4, starting transfers between devices, halo(): return (lax.ppermute(w, AXES, up), lax.ppermute(w, AXES, down))  15.1 us
    ppermute x4, waiting for transfers between devices, halo(): return (lax.ppermute(w, AXES, up), lax.ppermute(w, AXES, down))  15 us
    unnamed x58, local copies, waits for them, and re-layouts  14.8 us
  transfers between devices with their start and end apart: 8, of which 6 were waited for; matrix products, arithmetic and copies ran while one was open for 1% of the time, Pallas kernels for 5%

profile of v1, /device:TPU:1, one launch (start us, length us, event | category | flops | bytes accessed | tf_op | source)
XLA Modules:
  0.0 252.6 jit_solution(2370616982624858379)
XLA Ops:
  0.7 6.8 %fusion.2 = f32[256,512]{1,0:T(8,128)S(1)} fusion(f32[512,3072]{1,0:T(8,128)} %stored.9), kind=kOutput, calls=%fused_computation.2 | convolution fusion | flops 2415919104 | bytes 9961472 | tf_op jit(solution)/shard_map/dot_general | solution.py:23
  7.5 1.7 fusion
  9.3 2.6 %fusion.11 = f32[512,64]{1,0:T(8,128)S(1)} fusion(f32[512,3072]{1,0:T(8,128)S(1)} %copy-done, f32[64,3072]{1,0:T(8,128)S(1)} %copy-done.9), kind=kOutput, calls=%fused_computation.38 | convolution fusion | flops 603979776 | bytes 7208960 | tf_op jit(solution)/shard_map/dot_general | solution.py:23
  11.9 0.1 pad_maximum_fusion
  12.0 1.8 all_to_all.43
  13.8 11.5 %all-to-all-start = ((f32[128,1,1792]{2,1,0:T(1,128)}), f32[128,1,1792]{2,1,0:T(1,128)S(1)}, u32[]{:S(2)}, u32[]{:S(2)}) async-start(f32[128,1,1792]{2,1,0:T(1,128)} %all_to_all.43), calls=%async_computation | async-start | bytes 1835008 | tf_op jit(solution)/shard_map/all_to_all | solution.py:40
  25.5 0.1 reshape.98
  25.6 0.1 copy.24
  25.7 0.1 lt.113
  25.8 17.1 %all-to-all-done = f32[128,1,1792]{2,1,0:T(1,128)S(1)} async-done(((f32[128,1,1792]{2,1,0:T(1,128)}), f32[128,1,1792]{2,1,0:T(1,128)S(1)}, u32[]{:S(2)}, u32[]{:S(2)}) %all-to-all-start) | async-done | bytes 917536 | tf_op jit(solution)/shard_map/all_to_all | solution.py:40
  42.9 0.6 reduce_sum.107
  43.4 1.4 broadcast_in_dim.76
  44.8 4.5 %all-to-all-start.1 = ((f32[128,1,1792]{2,1,0:T(1,128)}), f32[128,1,1792]{2,1,0:T(1,128)S(1)}, u32[]{:S(2)}, u32[]{:S(2)}) async-start(f32[128,1,1792]{2,1,0:T(1,128)} %broadcast_in_dim.76), calls=%async_computation.1 | async-start | bytes 1835008 | tf_op jit(solution)/shard_map/all_to_all | solution.py:42
  49.4 0.1 convert_reduce_fusion
  49.5 0.1 convert_reduce_fusion.1
  49.6 0.2 select_reduce_fusion
  49.8 17.1 %all-to-all-done.1 = f32[128,1,1792]{2,1,0:T(1,128)S(1)} async-done(((f32[128,1,1792]{2,1,0:T(1,128)}), f32[128,1,1792]{2,1,0:T(1,128)S(1)}, u32[]{:S(2)}, u32[]{:S(2)}) %all-to-all-start.1) | async-done | bytes 917536 | tf_op jit(solution)/shard_map/all_to_all | solution.py:42
  66.9 3.3 %reduce.5 = f32[128,1792]{1,0:T(8,128)} reduce(f32[128,1,1792]{2,1,0:T(1,128)S(1)} %all-to-all-done.1, f32[]{:T(128)} %constant.83), dimensions={1}, to_apply=%all_to_all.34.reduce_sub_computation | reduce | bytes 1835012 | tf_op jit(solution)/shard_map/all_to_all | solution.py:42
  70.2 1.5 reshape.100.packed
  71.7 0.8 first.1
  72.5 1.8 slice-done.1
  74.3 0.2 copy-done.10
  74.5 2.2 project.3.mid.prev.refs_1_.refs_2_
  76.7 0.5 collective-permute-start
  77.2 7.1 %collective-permute-start.1 = (f32[64,3072]{1,0:T(8,128)S(1)}, f32[64,3072]{1,0:T(8,128)}, u32[]{:S(2)}, u32[]{:S(2)}) collective-permute-start(f32[64,3072]{1,0:T(8,128)S(1)} %project.3.mid.prev.refs_1_.refs_2_), channel_id=1, source_target_pairs={{1,0},{2,1},{3,2},{4,3},{5,4},{6,5},{7,6},{8,7},{9,8},{10,9},{11,1... | collective-permute-start | bytes 2359304 | tf_op jit(solution)/shard_map/ppermute | solution.py:378
  84.2 0.6 convert_reduce_fusion.2
  86.2 0.2 select_reduce_fusion.2
  86.4 1.3 compare_select_fusion.1
  87.7 0.1 concatenate.6.plan
  87.8 4.1 %copy-done.1 = f32[24,7,128,128]{3,2,1,0:T(8,128)S(1)} copy-done((f32[24,7,128,128]{3,2,1,0:T(8,128)S(1)}, f32[24,7,128,128]{3,2,1,0:T(8,128)}, u32[]{:S(2)}) %copy-start.1) | copy-done | bytes 11010072
  91.9 6.1 %near_op.2 = (f32[24,128,128]{2,1,0:T(8,128)S(1)}, bf16[168,128,256]{2,1,0:T(8,128)(2,1)S(1)}, f32[64,64]{1,0:T(8,128)S(1)}) custom-call(s32[1014]{0:T(1024)S(1)} %concatenate.6.plan, f32[168,128,128]{2,1,0:T(8,128)S(1)} %bitcast.22, f32[64,3072]{1,0:T(8,128)S(1)} %project.3.mid.prev.refs_1_.refs_2_), custom_call_target="tpu_custom_call" | custom-call | flops 2000000000 | bytes 12582912 | tf_op jit(solution)/shard_map/near_op/pallas_call | solution.py:151
  98.1 3.5 %collective-permute-done.left = f32[64,3072]{1,0:T(8,128)} collective-permute-done((f32[64,3072]{1,0:T(8,128)S(1)}, f32[64,3072]{1,0:T(8,128)}, u32[]{:S(2)}, u32[]{:S(2)}) %collective-permute-start) | collective-permute-done | bytes 786464 | tf_op jit(solution)/shard_map/ppermute | solution.py:378
  101.6 13.6 %far_op.2 = (f32[64,3072]{1,0:T(8,128)S(1)}, f32[128,384]{1,0:T(8,128)S(1)}) custom-call(s32[1014]{0:T(1024)S(1)} %concatenate.6.plan, bf16[168,128,256]{2,1,0:T(8,128)(2,1)S(1)} %get-tuple-element.24.halves, f32[512,3072]{1,0:T(8,128)S(1)} %bitcast.17, f32[64,3072]{1,0:T(8,128)} %collective-permute-done.left, f32[64,3072]{1,0:T(8,128)} %collective-permute-done.1.right, ...), custom_call_target="tpu_custom_call" | custom-call | flops 2000000000 | bytes 20971520 | tf_op jit(solution)/shard_map/far_op/pallas_call | solution.py:171
  115.2 0.9 copy-done.13
  116.1 0.2 copy.30
  116.3 20.0 %all_to_all.50 = f32[128,1,384]{2,1,0:T(1,128)S(1)} all-to-all(f32[128,1,384]{2,1,0:T(1,128)S(1)} %copy.30), channel_id=1, replica_groups=mesh['row'=4,'basis'=8,'rep'=4] {'row','basis','rep'}, dimensions={0} | all-to-all | bytes 393216 | tf_op jit(solution)/shard_map/all_to_all | solution.py:40
  136.3 0.2 reduce_sum.108
  136.5 0.8 broadcast_in_dim.77
  137.2 4.9 %all-to-all-start.3 = ((f32[128,1,384]{2,1,0:T(1,128)}), f32[128,1,384]{2,1,0:T(1,128)}, u32[]{:S(2)}, u32[]{:S(2)}) async-start(f32[128,1,384]{2,1,0:T(1,128)} %broadcast_in_dim.77), calls=%async_computation.3 | async-start | bytes 393216 | tf_op jit(solution)/shard_map/all_to_all | solution.py:42
  142.1 1.2 copy-done.5
  143.3 0.7 after_first.1.c3t
  144.1 8.5 %all-to-all-done.3 = f32[128,1,384]{2,1,0:T(1,128)} async-done(((f32[128,1,384]{2,1,0:T(1,128)}), f32[128,1,384]{2,1,0:T(1,128)}, u32[]{:S(2)}, u32[]{:S(2)}) %all-to-all-start.3) | async-done | bytes 196640 | tf_op jit(solution)/shard_map/all_to_all | solution.py:42
  152.5 0.9 copy.39
  153.5 1.4 copy-done.6
  154.9 4.4 %second.1 = (f32[64,512]{1,0:T(8,128)S(1)}, f32[64,128]{1,0:T(8,128)S(1)}, f32[192,512]{1,0:T(8,128)S(1)}) custom-call(f32[128,384]{1,0:T(8,128)S(1)} %bitcast.29, f32[512,512]{1,0:T(8,128)S(1)} %copy-done.6, f32[64,512]{1,0:T(8,128)S(1)} %after_first.1.c3t), custom_call_target="tpu_custom_call" | custom-call | flops 10000000000 | bytes 2097152 | tf_op jit(solution)/shard_map/second/pallas_call | solution.py:353
  159.3 2.2 project.4.mid.refs_1_
  161.5 0.4 collective-permute-start.2
  161.9 7.2 %collective-permute-start.3 = (f32[64,3072]{1,0:T(8,128)S(1)}, f32[64,3072]{1,0:T(8,128)S(1)}, u32[]{:S(2)}, u32[]{:S(2)}) collective-permute-start(f32[64,3072]{1,0:T(8,128)S(1)} %project.4.mid.refs_1_), channel_id=1, source_target_pairs={{1,0},{2,1},{3,2},{4,3},{5,4},{6,5},{7,6},{8,7},{9,8},{10,9},{11,1... | collective-permute-start | bytes 2359304 | tf_op jit(solution)/shard_map/ppermute | solution.py:378
  169.1 6.1 %near_op.3 = (f32[24,128,128]{2,1,0:T(8,128)S(1)}, bf16[168,128,256]{2,1,0:T(8,128)(2,1)S(1)}, f32[64,64]{1,0:T(8,128)S(1)}) custom-call(s32[1014]{0:T(1024)S(1)} %concatenate.6.plan, f32[168,128,128]{2,1,0:T(8,128)S(1)} %bitcast.25, f32[64,3072]{1,0:T(8,128)S(1)} %project.4.mid.refs_1_), custom_call_target="tpu_custom_call" | custom-call | flops 2000000000 | bytes 12582912 | tf_op jit(solution)/shard_map/near_op/pallas_call | solution.py:151
  175.2 11.5 %collective-permute-done.2.left = f32[64,3072]{1,0:T(8,128)S(1)} collective-permute-done((f32[64,3072]{1,0:T(8,128)S(1)}, f32[64,3072]{1,0:T(8,128)S(1)}, u32[]{:S(2)}, u32[]{:S(2)}) %collective-permute-start.2) | collective-permute-done | bytes 786464 | tf_op jit(solution)/shard_map/ppermute | solution.py:378
  186.7 12.8 %far_op.3 = (f32[64,3072]{1,0:T(8,128)S(1)}, f32[128,384]{1,0:T(8,128)S(1)}) custom-call(s32[1014]{0:T(1024)S(1)} %concatenate.6.plan, bf16[168,128,256]{2,1,0:T(8,128)(2,1)S(1)} %get-tuple-element.33.halves, f32[512,3072]{1,0:T(8,128)S(1)} %bitcast.19, f32[64,3072]{1,0:T(8,128)S(1)} %collective-permute-done.2.left, ...), custom_call_target="tpu_custom_call" | custom-call | flops 2000000000 | bytes 20971520 | tf_op jit(solution)/shard_map/far_op/pallas_call | solution.py:171
  199.6 0.9 copy-done.11
  200.4 0.2 copy.31
  200.6 19.6 %all_to_all.51 = f32[128,1,384]{2,1,0:T(1,128)S(1)} all-to-all(f32[128,1,384]{2,1,0:T(1,128)S(1)} %copy.31), channel_id=1, replica_groups=mesh['row'=4,'basis'=8,'rep'=4] {'row','basis','rep'}, dimensions={0} | all-to-all | bytes 393216 | tf_op jit(solution)/shard_map/all_to_all | solution.py:40
  220.3 0.2 reduce_sum.109
  220.4 0.8 broadcast_in_dim.78
  221.2 5.0 %all-to-all-start.5 = ((f32[128,1,384]{2,1,0:T(1,128)}), f32[128,1,384]{2,1,0:T(1,128)}, u32[]{:S(2)}, u32[]{:S(2)}) async-start(f32[128,1,384]{2,1,0:T(1,128)} %broadcast_in_dim.78), calls=%async_computation.5 | async-start | bytes 393216 | tf_op jit(solution)/shard_map/all_to_all | solution.py:42
  226.2 1.2 copy-done.7
  227.4 0.9 after.1.c3
  228.4 8.2 %all-to-all-done.5 = f32[128,1,384]{2,1,0:T(1,128)} async-done(((f32[128,1,384]{2,1,0:T(1,128)}), f32[128,1,384]{2,1,0:T(1,128)}, u32[]{:S(2)}, u32[]{:S(2)}) %all-to-all-start.5) | async-done | bytes 196640 | tf_op jit(solution)/shard_map/all_to_all | solution.py:42
  236.5 0.9 copy.38
  237.5 1.2 copy-done.8
  238.7 10.6 %third.1 = (f32[64,512]{1,0:T(8,128)S(1)}, f32[64,192]{1,0:T(8,128)S(1)}, f32[2,64,64]{2,1,0:T(8,128)}, f32[2,64,64]{2,1,0:T(8,128)}) custom-call(f32[128,384]{1,0:T(8,128)S(1)} %bitcast.27, f32[512,512]{1,0:T(8,128)S(1)} %copy-done.8, f32[64,640]{1,0:T(8,128)S(1)} %after.1.c3, f32[192,512]{1,0:T(8,128)S(1)} %get-tuple-element.37.keep), custom_call_target="tpu_custom_call" | custom-call | flops 10000000000 | bytes 2097152 | tf_op jit(solution)/shard_map/third/pallas_call | solution.py:353
  249.4 3.2 %project.5 = f32[64,3072]{1,0:T(8,128)} custom-call(f32[64,512]{1,0:T(8,128)S(1)} %get-tuple-element.40.cs, f32[64,192]{1,0:T(8,128)S(1)} %get-tuple-element.41.cw, f32[512,3072]{1,0:T(8,128)S(1)} %bitcast.21, f32[64,3072]{1,0:T(8,128)S(1)} %copy-done.12, f32[64,3072]{1,0:T(8,128)S(1)} %copy-done.3, f32[64,3072]{1,0:T(8,128)S(1)} %project.3.mid.prev.refs_1_.refs_2_), custom_call_target="tpu_custom_call" | custom-call | tf_op jit(solution)/shard_map/project/pallas_call | solution.py:233
  (62 shorter events, 0.3 us)
Async XLA Ops:
  0.6 6.9 %copy-start = (f32[512,3072]{1,0:T(8,128)S(1)}, f32[512,3072]{1,0:T(8,128)}, u32[]{:S(2)}) copy-start(f32[512,3072]{1,0:T(8,128)} %stored.9) | copy-start | bytes 18874372
  0.6 8.6 %copy-start.9 = (f32[64,3072]{1,0:T(8,128)S(1)}, f32[64,3072]{1,0:T(8,128)}, u32[]{:S(2)}) copy-start(f32[64,3072]{1,0:T(8,128)} %refs_0_.1) | copy-start | bytes 2359300
  9.2 16.1 %copy-start.15 = (s32[24,7]{0,1:T(8,128)S(1)}, s32[24,7]{0,1:T(8,128)}, u32[]{:S(2)}) copy-start(s32[24,7]{0,1:T(8,128)} %param.6) | copy-start | bytes 2020
  9.2 16.3 %copy-start.16 = (s32[24]{0:T(128)S(1)}, s32[24]{0:T(128)}, u32[]{:S(2)}) copy-start(s32[24]{0:T(128)} %param.7) | copy-start | bytes 292
  13.8 29.0 %all-to-all-start = ((f32[128,1,1792]{2,1,0:T(1,128)}), f32[128,1,1792]{2,1,0:T(1,128)S(1)}, u32[]{:S(2)}, u32[]{:S(2)}) async-start(f32[128,1,1792]{2,1,0:T(1,128)} %all_to_all.43), calls=%async_computation | async-start | bytes 1835008 | tf_op jit(solution)/shard_map/all_to_all | solution.py:40
  44.8 22.0 %all-to-all-start.1 = ((f32[128,1,1792]{2,1,0:T(1,128)}), f32[128,1,1792]{2,1,0:T(1,128)S(1)}, u32[]{:S(2)}, u32[]{:S(2)}) async-start(f32[128,1,1792]{2,1,0:T(1,128)} %broadcast_in_dim.76), calls=%async_computation.1 | async-start | bytes 1835008 | tf_op jit(solution)/shard_map/all_to_all | solution.py:42
  70.2 2.3 slice-start
  71.7 2.7 %slice-start.1 = ((s8[6291456]{0:T(1024)(128)(4,1)}), s8[4194304]{0:T(1024)(128)(4,1)S(1)}, s32[]{:S(2)}) async-start(s8[6291456]{0:T(1024)(128)(4,1)} %bitcast.14), calls=%async_computation.7 | async-start | bytes 8388608
  71.7 2.8 %copy-start.10 = (f32[64,3072]{1,0:T(8,128)S(1)}, f32[64,3072]{1,0:T(8,128)}, u32[]{:S(2)}) copy-start(f32[64,3072]{1,0:T(8,128)} %refs_0_.1) | copy-start | bytes 2359300
  72.5 4.2 %copy-start.4 = (f32[512,512]{1,0:T(8,128)}, f32[512,512]{1,0:T(8,128)S(1)}, u32[]{:S(2)}) copy-start(f32[512,512]{1,0:T(8,128)S(1)} %get-tuple-element.28.s) | copy-start | bytes 3145732
  76.7 24.9 %slice-start.2 = ((s8[6291456]{0:T(1024)(128)(4,1)}), s8[2097152]{0:T(1024)(128)(4,1)S(1)}, s32[]{:S(2)}) async-start(s8[6291456]{0:T(1024)(128)(4,1)} %bitcast.16), calls=%async_computation.8 | async-start | bytes 4194304
  76.7 24.9 %collective-permute-start = (f32[64,3072]{1,0:T(8,128)S(1)}, f32[64,3072]{1,0:T(8,128)}, u32[]{:S(2)}, u32[]{:S(2)}) collective-permute-start(f32[64,3072]{1,0:T(8,128)S(1)} %project.3.mid.prev.refs_1_.refs_2_), channel_id=1, source_target_pairs={{0,1},{1,2},{2,3},{3,4},{4,5},{5,6},{6,7},{7,8},{8,9},{9,10},{10,1... | collective-permute-start | bytes 2359304 | tf_op jit(solution)/shard_map/ppermute | solution.py:378
  77.2 24.4 %collective-permute-start.1 = (f32[64,3072]{1,0:T(8,128)S(1)}, f32[64,3072]{1,0:T(8,128)}, u32[]{:S(2)}, u32[]{:S(2)}) collective-permute-start(f32[64,3072]{1,0:T(8,128)S(1)} %project.3.mid.prev.refs_1_.refs_2_), channel_id=1, source_target_pairs={{1,0},{2,1},{3,2},{4,3},{5,4},{6,5},{7,6},{8,7},{9,8},{10,9},{11,1... | collective-permute-start | bytes 2359304 | tf_op jit(solution)/shard_map/ppermute | solution.py:378
  87.8 4.1 %copy-start.1 = (f32[24,7,128,128]{3,2,1,0:T(8,128)S(1)}, f32[24,7,128,128]{3,2,1,0:T(8,128)}, u32[]{:S(2)}) copy-start(f32[24,7,128,128]{3,2,1,0:T(8,128)} %param.5) | copy-start | bytes 33030148
  91.9 9.7 %slice-start.3 = ((s8[6291456]{0:T(1024)(128)(4,1)}), s8[4194304]{0:T(1024)(128)(4,1)S(1)}, s32[]{:S(2)}) async-start(s8[6291456]{0:T(1024)(128)(4,1)} %bitcast.16), calls=%async_computation.9 | async-start | bytes 8388608
  115.2 0.9 copy-start.13
  137.2 15.3 %all-to-all-start.3 = ((f32[128,1,384]{2,1,0:T(1,128)}), f32[128,1,384]{2,1,0:T(1,128)}, u32[]{:S(2)}, u32[]{:S(2)}) async-start(f32[128,1,384]{2,1,0:T(1,128)} %broadcast_in_dim.77), calls=%async_computation.3 | async-start | bytes 393216 | tf_op jit(solution)/shard_map/all_to_all | solution.py:42
  142.1 1.2 copy-start.5
  143.3 16.0 %slice-start.4 = ((s8[6291456]{0:T(1024)(128)(4,1)}), s8[2097152]{0:T(1024)(128)(4,1)S(1)}, s32[]{:S(2)}) async-start(s8[6291456]{0:T(1024)(128)(4,1)} %bitcast.18), calls=%async_computation.10 | async-start | bytes 4194304
  153.5 15.6 %slice-start.8 = ((s8[11010048]{0:T(1024)(128)(4,1)}), s8[4194304]{0:T(1024)(128)(4,1)S(1)}, s32[]{:S(2)}) async-start(s8[11010048]{0:T(1024)(128)(4,1)} %bitcast.23), calls=%async_computation.14 | async-start | bytes 8388608
  153.5 1.4 copy-start.6
  154.9 4.4 %slice-start.5 = ((s8[6291456]{0:T(1024)(128)(4,1)}), s8[4194304]{0:T(1024)(128)(4,1)S(1)}, s32[]{:S(2)}) async-start(s8[6291456]{0:T(1024)(128)(4,1)} %bitcast.18), calls=%async_computation.11 | async-start | bytes 8388608
  154.9 4.4 %copy-start.14 = (f32[64,3072]{1,0:T(8,128)S(1)}, f32[64,3072]{1,0:T(8,128)}, u32[]{:S(2)}) copy-start(f32[64,3072]{1,0:T(8,128)} %copy-done.13) | copy-start | bytes 2359300
  154.9 14.2 %slice-start.9 = ((s8[11010048]{0:T(1024)(128)(4,1)}), s8[4194304]{0:T(1024)(128)(4,1)S(1)}, s32[]{:S(2)}) async-start(s8[11010048]{0:T(1024)(128)(4,1)} %bitcast.23), calls=%async_computation.15 | async-start | bytes 8388608
  154.9 14.2 %slice-start.10 = ((s8[11010048]{0:T(1024)(128)(4,1)}), s8[2621440]{0:T(1024)(128)(4,1)S(1)}, s32[]{:S(2)}) async-start(s8[11010048]{0:T(1024)(128)(4,1)} %bitcast.23), calls=%async_computation.16 | async-start | bytes 5242880
  161.5 38.0 %copy-start.2 = (f32[64,3072]{1,0:T(8,128)}, f32[64,3072]{1,0:T(8,128)S(1)}, u32[]{:S(2)}) copy-start(f32[64,3072]{1,0:T(8,128)S(1)} %project.4.mid.refs_1_) | copy-start | bytes 2359300
  161.5 25.2 %collective-permute-start.2 = (f32[64,3072]{1,0:T(8,128)S(1)}, f32[64,3072]{1,0:T(8,128)S(1)}, u32[]{:S(2)}, u32[]{:S(2)}) collective-permute-start(f32[64,3072]{1,0:T(8,128)S(1)} %project.4.mid.refs_1_), channel_id=1, source_target_pairs={{0,1},{1,2},{2,3},{3,4},{4,5},{5,6},{6,7},{7,8},{8,9},{9,10},{10,1... | collective-permute-start | bytes 2359304 | tf_op jit(solution)/shard_map/ppermute | solution.py:378
  161.9 24.8 %collective-permute-start.3 = (f32[64,3072]{1,0:T(8,128)S(1)}, f32[64,3072]{1,0:T(8,128)S(1)}, u32[]{:S(2)}, u32[]{:S(2)}) collective-permute-start(f32[64,3072]{1,0:T(8,128)S(1)} %project.4.mid.refs_1_), channel_id=1, source_target_pairs={{1,0},{2,1},{3,2},{4,3},{5,4},{6,5},{7,6},{8,7},{9,8},{10,9},{11,1... | collective-permute-start | bytes 2359304 | tf_op jit(solution)/shard_map/ppermute | solution.py:378
  199.6 0.9 copy-start.11
  221.2 28.1 %slice-start.6 = ((s8[6291456]{0:T(1024)(128)(4,1)}), s8[2097152]{0:T(1024)(128)(4,1)S(1)}, s32[]{:S(2)}) async-start(s8[6291456]{0:T(1024)(128)(4,1)} %bitcast.20), calls=%async_computation.12 | async-start | bytes 4194304
  221.2 15.3 %all-to-all-start.5 = ((f32[128,1,384]{2,1,0:T(1,128)}), f32[128,1,384]{2,1,0:T(1,128)}, u32[]{:S(2)}, u32[]{:S(2)}) async-start(f32[128,1,384]{2,1,0:T(1,128)} %broadcast_in_dim.78), calls=%async_computation.5 | async-start | bytes 393216 | tf_op jit(solution)/shard_map/all_to_all | solution.py:42
  226.2 1.2 copy-start.7
  237.5 1.2 copy-start.8
  238.7 10.6 %slice-start.7 = ((s8[6291456]{0:T(1024)(128)(4,1)}), s8[4194304]{0:T(1024)(128)(4,1)S(1)}, s32[]{:S(2)}) async-start(s8[6291456]{0:T(1024)(128)(4,1)} %bitcast.20), calls=%async_computation.13 | async-start | bytes 8388608
  238.7 10.6 %copy-start.3 = (f32[64,3072]{1,0:T(8,128)S(1)}, f32[64,3072]{1,0:T(8,128)}, u32[]{:S(2)}) copy-start(f32[64,3072]{1,0:T(8,128)} %copy-done.2) | copy-start | bytes 2359300
  238.7 10.7 %copy-start.12 = (f32[64,3072]{1,0:T(8,128)S(1)}, f32[64,3072]{1,0:T(8,128)}, u32[]{:S(2)}) copy-start(f32[64,3072]{1,0:T(8,128)} %copy-done.11) | copy-start | bytes 2359300

commit v2 on v1

--- a/solution.py
+++ b/solution.py
@@ -36,11 +36,9 @@
 
 
 def total(x):
-    n = lax.axis_size(AXES)
-    parts = lax.all_to_all(x.reshape(n, x.size // n), AXES, 0, 0, tiled=True)
-    mine = jnp.sum(parts, axis=0)
-    out = lax.all_to_all(jnp.broadcast_to(mine[None], parts.shape), AXES, 0, 0, tiled=True)
-    return out.reshape(x.shape)
+    parts = lax.all_to_all(x, AXES, 0, 0, tiled=True)
+    mine = jnp.sum(parts, axis=0, keepdims=True)
+    return lax.all_to_all(jnp.broadcast_to(mine, x.shape), AXES, 0, 0, tiled=True)[:, 0]
 
 
 def split(x):
@@ -49,39 +47,36 @@
     return hi, lo
 
 
-def turned(x):
-    hi = x.astype(BF16).astype(F32)
-    return jnp.concatenate([hi, x - hi], axis=0).T.astype(BF16)
-
-
-def add_slots(plan, first, chunks, size, blocks, pieces, tot):
+def stacked(x):
+    return jnp.concatenate(split(x), axis=0)
+
+
+def bdot_nt(a, b):
+    return lax.dot_general(a, b, (((1,), (1,)), ((), ())), preferred_element_type=F32)
+
+
+def add_slots(plan, first, chunks, size, halves, pieces, tot):
     @pl.loop(0, chunks)
     def _(c):
         parts = []
         for e in range(CHUNK):
             at = first + c * CHUNK + e
-            parts.append((plan[at + size], bdot(blocks[plan[at]], pieces[plan[at + 2 * size]])))
+            v = pieces[plan[at + 2 * size]]
+            parts.append((plan[at + size], bdot_nt(jnp.concatenate([v, v], axis=1), halves[plan[at]])))
         for row, part in parts:
             tot[row] += part
 
 
-def put_piece(pieces, at, x):
-    bs = x.shape[1]
-    t = turned(x)
-    pieces[at, :bs] = t
-    pieces[at, bs:] = t
-
-
 def near_kernel(plan, blocks, mid, tot, halves, gram, pieces):
-    nbd, bs, _ = tot.shape
-    bw = mid.shape[0]
+    nbd, _, bs = tot.shape
+    bw, n = mid.shape
     size = plan.shape[0] // 6
-    pieces[nbd] = jnp.zeros((2 * bs, 2 * bw), BF16)
+    pieces[nbd] = jnp.zeros((2 * bw, bs), BF16)
     tot[...] = jnp.zeros_like(tot)
 
     @pl.loop(0, nbd, unroll=4)
     def _(b):
-        put_piece(pieces, b, mid[:, pl.ds(pl.multiple_of(b * bs, bs), bs)])
+        pieces[b] = stacked(mid[:, pl.ds(pl.multiple_of(b * bs, bs), bs)])
 
     @pl.loop(0, blocks.shape[0], unroll=4)
     def _(k):
@@ -89,56 +84,54 @@
 
     add_slots(plan, 1, plan[0], size, halves, pieces, tot)
     g = jnp.zeros((bw, 2 * bw), F32)
-    for b in range(0, nbd, RB):
-        hi, lo = split(mid[:, b * bs : (b + RB) * bs])
-        w = jnp.concatenate([pieces[b + r, :bs] for r in range(RB)], axis=0)
-        g = g + bdot(hi, w) + bdot(lo, w)
+    for b in range(0, n, TILE):
+        hi, lo = split(mid[:, b : b + TILE])
+        w = jnp.concatenate([hi, lo], axis=0)
+        g = g + bdot_nt(hi, w) + bdot_nt(lo, w)
     gram[...] = g[:, :bw] + g[:, bw:]
 
 
-def far_kernel(plan, halves, stored, left, right, near, mid, prev, gram, u_out, m_out, tot, pieces, ut, acc, accw):
-    nbd, bs, _ = tot.shape
+def far_kernel(plan, halves, stored, left, right, near, mid, prev, gram, u_out, m_out, tot, pieces, acc, accw):
+    nbd, _, bs = tot.shape
     bw, n = mid.shape
     ks = stored.shape[0]
     size = plan.shape[0] // 6
-    pieces[2 * nbd] = jnp.zeros((2 * bs, 2 * bw), BF16)
+    pieces[2 * nbd] = jnp.zeros((2 * bw, bs), BF16)
     for k, src in enumerate((left, right)):
 
         @pl.loop(0, nbd, unroll=4)
         def _(b):
-            put_piece(pieces, k * nbd + b, src[:, pl.ds(pl.multiple_of(b * bs, bs), bs)])
+            pieces[k * nbd + b] = stacked(src[:, pl.ds(pl.multiple_of(b * bs, bs), bs)])
 
     tot[...] = jnp.zeros_like(tot)
     add_slots(plan, 3 * size + 1, plan[3 * size], size, halves, pieces, tot)
-
-    @pl.loop(0, nbd, unroll=RB)
-    def _(b):
-        here = pl.ds(pl.multiple_of(b * bs, bs), bs)
-        t = (tot[b] + near[b]).T
-        u = t[:bw] + t[bw:]
-        u_out[:, here] = u
-        ut[here] = turned(u)
-
     acc[...] = jnp.zeros_like(acc)
     accw[...] = jnp.zeros_like(accw)
+    per = TILE // bs
 
     @pl.loop(0, n // TILE)
     def _(b):
         here = pl.ds(pl.multiple_of(b * TILE, TILE), TILE)
-        t = ut[here]
+        us = []
+        for r in range(per):
+            t = tot[b * per + r] + near[b * per + r]
+            us.append(t[:bw] + t[bw:])
+        u = jnp.concatenate(us, axis=1)
+        u_out[:, here] = u
+        u2 = stacked(u)
         shi, slo = split(stored[:, here])
-        acc[...] += bdot(shi, t) + bdot(slo, t)
-        rhi, rlo = split(jnp.concatenate([mid[:, here], prev[:, here], u_out[:, here]], axis=0))
-        accw[...] += bdot(rhi, t) + bdot(rlo, t)
+        acc[...] += bdot_nt(shi, u2) + bdot_nt(slo, u2)
+        rhi, rlo = split(jnp.concatenate([mid[:, here], prev[:, here], u], axis=0))
+        accw[...] += bdot_nt(rhi, u2) + bdot_nt(rlo, u2)
 
     t = acc[...].T
     a = t[:bw] + t[bw:]
-    m_out[:bw, : ks // 2] = a[:, : ks // 2]
-    m_out[bw:, : ks // 2] = a[:, ks // 2 :]
+    m_out[:bw, 0, : ks // 2] = a[:, : ks // 2]
+    m_out[bw:, 0, : ks // 2] = a[:, ks // 2 :]
     w = accw[...]
     w = w[:, :bw] + w[:, bw:]
-    m_out[:bw, ks // 2 :] = jnp.concatenate([w[:bw], gram[...]], axis=1)
-    m_out[bw:, ks // 2 :] = jnp.concatenate([w[bw : 2 * bw], w[2 * bw :]], axis=1)
+    m_out[:bw, 0, ks // 2 :] = jnp.concatenate([w[:bw], gram[...]], axis=1)
+    m_out[bw:, 0, ks // 2 :] = jnp.concatenate([w[bw : 2 * bw], w[2 * bw :]], axis=1)
 
 
 VMEM = pl.BlockSpec(memory_space=pltpu.VMEM)
@@ -153,11 +146,11 @@
         in_specs=[SMEM, VMEM, VMEM],
         out_specs=[VMEM] * 3,
         out_shape=[
-            jax.ShapeDtypeStruct((nbd, bs, 2 * bw), F32),
+            jax.ShapeDtypeStruct((nbd, 2 * bw, bs), F32),
             jax.ShapeDtypeStruct((blocks.shape[0], bs, 2 * bs), BF16),
             jax.ShapeDtypeStruct((bw, bw), F32),
         ],
-        scratch_shapes=[pltpu.VMEM((nbd + 1, 2 * bs, 2 * bw), BF16)],
+        scratch_shapes=[pltpu.VMEM((nbd + 1, 2 * bw, bs), BF16)],
         compiler_params=pltpu.CompilerParams(vmem_limit_bytes=VMEM_LIMIT),
         cost_estimate=pl.CostEstimate(flops=2 * 10**9, bytes_accessed=12 * 2**20, transcendentals=0),
         name="near_op",
@@ -165,7 +158,7 @@
 
 
 def far_op(plan, halves, stored, left, right, near, mid, prev, gram):
-    nbd, bs, _ = near.shape
+    nbd, _, bs = near.shape
     bw, n = mid.shape
     ks = stored.shape[0]
     return pl.pallas_call(
@@ -173,15 +166,14 @@
         in_specs=[SMEM] + [VMEM] * 8,
         out_specs=[VMEM] * 2,
         scratch_shapes=[
-            pltpu.VMEM((nbd, bs, 2 * bw), F32),
-            pltpu.VMEM((2 * nbd + 1, 2 * bs, 2 * bw), BF16),
-            pltpu.VMEM((n, 2 * bw), BF16),
+            pltpu.VMEM((nbd, 2 * bw, bs), F32),
+            pltpu.VMEM((2 * nbd + 1, 2 * bw, bs), BF16),
             pltpu.VMEM((ks, 2 * bw), F32),
             pltpu.VMEM((3 * bw, 2 * bw), F32),
         ],
         out_shape=[
             jax.ShapeDtypeStruct((bw, n), F32),
-            jax.ShapeDtypeStruct((2 * bw, ks // 2 + 2 * bw), F32),
+            jax.ShapeDtypeStruct((2 * bw, 1, ks // 2 + 2 * bw), F32),
         ],
         compiler_params=pltpu.CompilerParams(vmem_limit_bytes=VMEM_LIMIT),
         cost_estimate=pl.CostEstimate(flops=2 * 10**9, bytes_accessed=20 * 2**20, transcendentals=0),
@@ -275,9 +267,12 @@
     return mst, a[:, :bw], a[:, bw:], b[:, :bw], b[:, bw:]
 
 
-def first_kernel(packed, s, c1t_out, minus_dt):
-    half = packed.shape[0]
-    bw = c1t_out.shape[0]
+def first_kernel(t, s, c1t_out, minus_dt):
+    bw, ks = c1t_out.shape
+    half = ks // 2
+    packed = t[...]
+    cut = packed.shape[1] // 2
+    packed = jnp.concatenate([packed[:, :cut], packed[:, cut:]], axis=0)
     s12 = packed[:, half : 2 * half]
     s[:half] = packed[:, : 2 * half]
     s[half:] = jnp.concatenate([s12.T, packed[:, 2 * half : 3 * half]], axis=1)
@@ -363,7 +358,6 @@
     nbd, slots, bs, _ = blocks.shape
     bw, n = start_block.shape
     ks = stored.shape[0]
-    half = ks // 2
     devices = lax.axis_size(AXES)
     position = lax.axis_index(AXES)
     nb = nbd * devices
@@ -377,10 +371,13 @@
     def halo(w):
         return lax.ppermute(w, AXES, up), lax.ppermute(w, AXES, down)
 
+    half = ks // 2
     top = dot_nt(stored[:half], stored, HIGH)
     corner = dot_nt(stored[half:], stored[half:], HIGH)
     first = dot_nt(stored, start_block, HIGH)
-    packed = total(jnp.concatenate([top, corner, first[:half], first[half:]], axis=1))
+    packed = jnp.concatenate([top, corner, first[:half], first[half:]], axis=1)
+    packed = jnp.concatenate([packed[:devices], packed[devices:]], axis=1)
+    packed = total(packed[:, None, :])
     wide = (bw, ks)
     s, c1t, minus_dt = small(first_kernel, "first", [(ks, ks), wide, wide], packed)
     w1 = project(minus_dt, jnp.eye(bw, dtype=F32), stored, start_block)

time: 250 us -> 239 us (0.956)
  Pallas kernels: 63.7 us -> 58.9 us
  other arithmetic: 6.89 us -> 3.65 us
    pallas_call x2, Pallas kernels: 26.4 us -> 19.4 us  [far_op(): pl.pallas_call(far_kernel, in_specs=[SMEM] + [VMEM] * 8, out_specs=[VMEM]...]
    all_to_all x1 -> x0, other arithmetic: 3.3 us -> none  [total(): lax.all_to_all(jnp.broadcast_to(mine[None], parts.shape), AXES, 0, 0, til...]
    unnamed x58 -> x57, local copies, waits for them, and re-layouts: 14.8 us -> 15.3 us
  transfers between devices with their start and end apart: 8 -> 8, of which waited for: 6 -> 6; matrix products, arithmetic and copies ran while one was open for 1% -> 1% of each run, Pallas kernels for 5% -> 7%
where the time goes in v2:
time: 239 us; the launch traced here: 241 us
  waiting for transfers between devices  63.8 us (27%)
  Pallas kernels  58.9 us (25%)
  starting transfers between devices  40.9 us (17%)
  blocking collectives  39.1 us (16%)
  local copies, waits for them, and re-layouts  20.7 us (9%)
  matrix products  11.1 us (5%)
  other arithmetic  3.65 us (2%)
  between operations  2.45 us (1%)
    all_to_all x2, blocking collectives, total(): parts = lax.all_to_all(x, AXES, 0, 0, tiled=True)  39.1 us
    all_to_all x3, waiting for transfers between devices, total(): lax.all_to_all(jnp.broadcast_to(mine, x.shape), AXES, 0, 0, tiled=True)  33.8 us
    pallas_call x2, Pallas kernels, far_op(): pl.pallas_call(far_kernel, in_specs=[SMEM] + [VMEM] * 8, out_specs=[VMEM]...  19.4 us
    pallas_call x5, Pallas kernels, small(): pl.pallas_call(kernel, out_shape=[jax.ShapeDtypeStruct(s, F32) for s in s...  17.5 us
    all_to_all x1, waiting for transfers between devices, total(): parts = lax.all_to_all(x, AXES, 0, 0, tiled=True)  17.1 us
    unnamed x57, local copies, waits for them, and re-layouts  15.3 us
    ppermute x4, starting transfers between devices, halo(): return (lax.ppermute(w, AXES, up), lax.ppermute(w, AXES, down))  15.1 us
    pallas_call x2, Pallas kernels, near_op(): pl.pallas_call(near_kernel, in_specs=[SMEM, VMEM, VMEM], out_specs=[VMEM]...  14.4 us
  transfers between devices with their start and end apart: 8, of which 6 were waited for; matrix products, arithmetic and copies ran while one was open for 1% of the time, Pallas kernels for 7%

profile of v2, /device:TPU:1, one launch (start us, length us, event | category | flops | bytes accessed | tf_op | source)
XLA Modules:
  0.0 240.6 jit_solution(6112559157366961194)
XLA Ops:
  0.7 6.8 %fusion.2 = f32[256,512]{1,0:T(8,128)S(1)} fusion(f32[512,3072]{1,0:T(8,128)} %stored.9), kind=kOutput, calls=%fused_computation.2 | convolution fusion | flops 2415919104 | bytes 9961472 | tf_op jit(solution)/shard_map/dot_general | solution.py:23
  7.5 1.7 fusion
  9.2 2.6 %fusion.12 = f32[512,64]{1,0:T(8,128)S(1)} fusion(f32[512,3072]{1,0:T(8,128)S(1)} %copy-done, f32[64,3072]{1,0:T(8,128)S(1)} %copy-done.9), kind=kOutput, calls=%fused_computation.41 | convolution fusion | flops 603979776 | bytes 7208960 | tf_op jit(solution)/shard_map/dot_general | solution.py:23
  11.9 0.1 pad_maximum_fusion
  12.0 0.1 fusion.10
  12.1 0.1 maximum_bitcast_fusion
  12.1 1.9 copy.27
  14.0 11.5 %all-to-all-start = ((f32[128,1,1792]{2,1,0:T(1,128)}), f32[128,1,1792]{2,1,0:T(1,128)S(1)}, u32[]{:S(2)}, u32[]{:S(2)}) async-start(f32[128,1,1792]{2,1,0:T(1,128)} %copy.27), calls=%async_computation | async-start | bytes 1835008 | tf_op jit(solution)/shard_map/all_to_all | solution.py:39
  25.6 0.1 copy.23
  25.7 0.1 reshape.83
  25.8 0.1 copy.22
  25.9 0.1 lt.113
  26.0 17.1 %all-to-all-done = f32[128,1,1792]{2,1,0:T(1,128)S(1)} async-done(((f32[128,1,1792]{2,1,0:T(1,128)}), f32[128,1,1792]{2,1,0:T(1,128)S(1)}, u32[]{:S(2)}, u32[]{:S(2)}) %all-to-all-start) | async-done | bytes 917536 | tf_op jit(solution)/shard_map/all_to_all | solution.py:39
  43.1 0.6 reduce_sum.107
  43.6 1.4 broadcast_in_dim.80
  45.0 4.5 %all-to-all-start.1 = ((f32[128,1,1792]{2,1,0:T(1,128)}), f32[128,1,1792]{2,1,0:T(1,128)S(1)}, u32[]{:S(2)}, u32[]{:S(2)}) async-start(f32[128,1,1792]{2,1,0:T(1,128)} %broadcast_in_dim.80), calls=%async_computation.1 | async-start | bytes 1835008 | tf_op jit(solution)/shard_map/all_to_all | solution.py:41
  49.6 0.1 convert_reduce_fusion
  49.7 0.1 convert_reduce_fusion.1
  49.8 0.2 select_reduce_fusion
  50.0 17.1 %all-to-all-done.1 = f32[128,1,1792]{2,1,0:T(1,128)S(1)} async-done(((f32[128,1,1792]{2,1,0:T(1,128)}), f32[128,1,1792]{2,1,0:T(1,128)S(1)}, u32[]{:S(2)}, u32[]{:S(2)}) %all-to-all-start.1) | async-done | bytes 917536 | tf_op jit(solution)/shard_map/all_to_all | solution.py:41
  67.1 0.1 copy.36
  67.1 0.8 first.1
  68.0 1.7 slice-done
  69.6 0.7 slice-done.1
  70.3 2.2 project.3.mid.prev.refs_1_.refs_2_
  72.5 0.5 collective-permute-start
  73.0 7.1 %collective-permute-start.1 = (f32[64,3072]{1,0:T(8,128)S(1)}, f32[64,3072]{1,0:T(8,128)}, u32[]{:S(2)}, u32[]{:S(2)}) collective-permute-start(f32[64,3072]{1,0:T(8,128)S(1)} %project.3.mid.prev.refs_1_.refs_2_), channel_id=1, source_target_pairs={{1,0},{2,1},{3,2},{4,3},{5,4},{6,5},{7,6},{8,7},{9,8},{10,9},{11,1... | collective-permute-start | bytes 2359304 | tf_op jit(solution)/shard_map/ppermute | solution.py:372
  80.1 0.6 convert_reduce_fusion.2
  82.1 0.2 select_reduce_fusion.2
  82.2 1.3 compare_select_fusion.1
  83.6 0.1 concatenate.9.plan
  83.7 4.1 %copy-done.1 = f32[24,7,128,128]{3,2,1,0:T(8,128)S(1)} copy-done((f32[24,7,128,128]{3,2,1,0:T(8,128)S(1)}, f32[24,7,128,128]{3,2,1,0:T(8,128)}, u32[]{:S(2)}) %copy-start.1) | copy-done | bytes 11010072
  87.8 7.2 %near_op.2 = (f32[24,128,128]{2,1,0:T(8,128)S(1)}, bf16[168,128,256]{2,1,0:T(8,128)(2,1)S(1)}, f32[64,64]{1,0:T(8,128)S(1)}) custom-call(s32[1014]{0:T(1024)S(1)} %concatenate.9.plan, f32[168,128,128]{2,1,0:T(8,128)S(1)} %bitcast.25, f32[64,3072]{1,0:T(8,128)S(1)} %project.3.mid.prev.refs_1_.refs_2_), custom_call_target="tpu_custom_call" | custom-call | flops 2000000000 | bytes 12582912 | tf_op jit(solution)/shard_map/near_op/pallas_call | solution.py:144
  95.0 2.5 %collective-permute-done.left = f32[64,3072]{1,0:T(8,128)} collective-permute-done((f32[64,3072]{1,0:T(8,128)S(1)}, f32[64,3072]{1,0:T(8,128)}, u32[]{:S(2)}, u32[]{:S(2)}) %collective-permute-start) | collective-permute-done | bytes 786464 | tf_op jit(solution)/shard_map/ppermute | solution.py:372
  97.5 10.1 %far_op.2 = (f32[64,3072]{1,0:T(8,128)S(1)}, f32[128,1,384]{2,1,0:T(1,128)S(1)}) custom-call(s32[1014]{0:T(1024)S(1)} %concatenate.9.plan, bf16[168,128,256]{2,1,0:T(8,128)(2,1)S(1)} %get-tuple-element.24.halves, f32[512,3072]{1,0:T(8,128)S(1)} %bitcast.20, f32[64,3072]{1,0:T(8,128)} %collective-permute-done.left, f32[64,3072]{1,0:T(8,128)} %collective-permute-done.1.right, ...), custom_call_target="tpu_custom_call" | custom-call | flops 2000000000 | bytes 20971520 | tf_op jit(solution)/shard_map/far_op/pallas_call | solution.py:164
  107.6 0.9 copy-done.12
  108.5 19.8 %all_to_all.30 = f32[128,1,384]{2,1,0:T(1,128)S(1)} all-to-all(f32[128,1,384]{2,1,0:T(1,128)S(1)} %get-tuple-element.27), channel_id=1, replica_groups=mesh['row'=4,'basis'=8,'rep'=4] {'row','basis','rep'}, dimensions={0} | all-to-all | bytes 393216 | tf_op jit(solution)/shard_map/all_to_all | solution.py:39
  128.2 0.2 reduce_sum.108
  128.4 0.8 broadcast_in_dim.81
  129.2 4.9 %all-to-all-start.3 = ((f32[128,1,384]{2,1,0:T(1,128)}), f32[128,1,384]{2,1,0:T(1,128)}, u32[]{:S(2)}, u32[]{:S(2)}) async-start(f32[128,1,384]{2,1,0:T(1,128)} %broadcast_in_dim.81), calls=%async_computation.3 | async-start | bytes 393216 | tf_op jit(solution)/shard_map/all_to_all | solution.py:41
  134.1 1.2 copy-done.5
  135.3 0.7 after_first.1.c3t
  136.0 8.5 %all-to-all-done.3 = f32[128,1,384]{2,1,0:T(1,128)} async-done(((f32[128,1,384]{2,1,0:T(1,128)}), f32[128,1,384]{2,1,0:T(1,128)}, u32[]{:S(2)}, u32[]{:S(2)}) %all-to-all-start.3) | async-done | bytes 196640 | tf_op jit(solution)/shard_map/all_to_all | solution.py:41
  144.5 0.9 copy.38
  145.4 1.4 copy-done.6
  146.8 4.4 %second.1 = (f32[64,512]{1,0:T(8,128)S(1)}, f32[64,128]{1,0:T(8,128)S(1)}, f32[192,512]{1,0:T(8,128)S(1)}) custom-call(f32[128,384]{1,0:T(8,128)S(1)} %bitcast.31, f32[512,512]{1,0:T(8,128)S(1)} %copy-done.6, f32[64,512]{1,0:T(8,128)S(1)} %after_first.1.c3t), custom_call_target="tpu_custom_call" | custom-call | flops 10000000000 | bytes 2097152 | tf_op jit(solution)/shard_map/second/pallas_call | solution.py:348
  151.3 2.2 project.4.mid.refs_1_
  153.5 0.4 collective-permute-start.2
  153.9 7.2 %collective-permute-start.3 = (f32[64,3072]{1,0:T(8,128)S(1)}, f32[64,3072]{1,0:T(8,128)S(1)}, u32[]{:S(2)}, u32[]{:S(2)}) collective-permute-start(f32[64,3072]{1,0:T(8,128)S(1)} %project.4.mid.refs_1_), channel_id=1, source_target_pairs={{1,0},{2,1},{3,2},{4,3},{5,4},{6,5},{7,6},{8,7},{9,8},{10,9},{11,1... | collective-permute-start | bytes 2359304 | tf_op jit(solution)/shard_map/ppermute | solution.py:372
  161.0 7.2 %near_op.3 = (f32[24,128,128]{2,1,0:T(8,128)S(1)}, bf16[168,128,256]{2,1,0:T(8,128)(2,1)S(1)}, f32[64,64]{1,0:T(8,128)S(1)}) custom-call(s32[1014]{0:T(1024)S(1)} %concatenate.9.plan, f32[168,128,128]{2,1,0:T(8,128)S(1)} %bitcast.28, f32[64,3072]{1,0:T(8,128)S(1)} %project.4.mid.refs_1_), custom_call_target="tpu_custom_call" | custom-call | flops 2000000000 | bytes 12582912 | tf_op jit(solution)/shard_map/near_op/pallas_call | solution.py:144
  168.3 10.4 %collective-permute-done.2.left = f32[64,3072]{1,0:T(8,128)S(1)} collective-permute-done((f32[64,3072]{1,0:T(8,128)S(1)}, f32[64,3072]{1,0:T(8,128)S(1)}, u32[]{:S(2)}, u32[]{:S(2)}) %collective-permute-start.2) | collective-permute-done | bytes 786464 | tf_op jit(solution)/shard_map/ppermute | solution.py:372
  178.7 9.3 %far_op.3 = (f32[64,3072]{1,0:T(8,128)S(1)}, f32[128,1,384]{2,1,0:T(1,128)S(1)}) custom-call(s32[1014]{0:T(1024)S(1)} %concatenate.9.plan, bf16[168,128,256]{2,1,0:T(8,128)(2,1)S(1)} %get-tuple-element.33.halves, f32[512,3072]{1,0:T(8,128)S(1)} %bitcast.22, f32[64,3072]{1,0:T(8,128)S(1)} %collective-permute-done.2.left, ...), custom_call_target="tpu_custom_call" | custom-call | flops 2000000000 | bytes 20971520 | tf_op jit(solution)/shard_map/far_op/pallas_call | solution.py:164
  188.0 0.9 copy-done.10
  188.9 19.3 %all_to_all.31 = f32[128,1,384]{2,1,0:T(1,128)S(1)} all-to-all(f32[128,1,384]{2,1,0:T(1,128)S(1)} %get-tuple-element.36), channel_id=1, replica_groups=mesh['row'=4,'basis'=8,'rep'=4] {'row','basis','rep'}, dimensions={0} | all-to-all | bytes 393216 | tf_op jit(solution)/shard_map/all_to_all | solution.py:39
  208.2 0.2 reduce_sum.109
  208.3 0.8 broadcast_in_dim.82
  209.1 5.0 %all-to-all-start.5 = ((f32[128,1,384]{2,1,0:T(1,128)}), f32[128,1,384]{2,1,0:T(1,128)}, u32[]{:S(2)}, u32[]{:S(2)}) async-start(f32[128,1,384]{2,1,0:T(1,128)} %broadcast_in_dim.82), calls=%async_computation.5 | async-start | bytes 393216 | tf_op jit(solution)/shard_map/all_to_all | solution.py:41
  214.2 1.2 copy-done.7
  215.4 0.9 after.1.c3
  216.3 8.3 %all-to-all-done.5 = f32[128,1,384]{2,1,0:T(1,128)} async-done(((f32[128,1,384]{2,1,0:T(1,128)}), f32[128,1,384]{2,1,0:T(1,128)}, u32[]{:S(2)}, u32[]{:S(2)}) %all-to-all-start.5) | async-done | bytes 196640 | tf_op jit(solution)/shard_map/all_to_all | solution.py:41
  224.6 0.9 copy.37
  225.5 1.2 copy-done.8
  226.7 10.6 %third.1 = (f32[64,512]{1,0:T(8,128)S(1)}, f32[64,192]{1,0:T(8,128)S(1)}, f32[2,64,64]{2,1,0:T(8,128)}, f32[2,64,64]{2,1,0:T(8,128)}) custom-call(f32[128,384]{1,0:T(8,128)S(1)} %bitcast.30, f32[512,512]{1,0:T(8,128)S(1)} %copy-done.8, f32[64,640]{1,0:T(8,128)S(1)} %after.1.c3, f32[192,512]{1,0:T(8,128)S(1)} %get-tuple-element.37.keep), custom_call_target="tpu_custom_call" | custom-call | flops 10000000000 | bytes 2097152 | tf_op jit(solution)/shard_map/third/pallas_call | solution.py:348
  237.4 3.2 %project.5 = f32[64,3072]{1,0:T(8,128)} custom-call(f32[64,512]{1,0:T(8,128)S(1)} %get-tuple-element.40.cs, f32[64,192]{1,0:T(8,128)S(1)} %get-tuple-element.41.cw, f32[512,3072]{1,0:T(8,128)S(1)} %bitcast.24, f32[64,3072]{1,0:T(8,128)S(1)} %copy-done.11, f32[64,3072]{1,0:T(8,128)S(1)} %copy-done.3, f32[64,3072]{1,0:T(8,128)S(1)} %project.3.mid.prev.refs_1_.refs_2_), custom_call_target="tpu_custom_call" | custom-call | tf_op jit(solution)/shard_map/project/pallas_call | solution.py:225
  (59 shorter events, 0.2 us)
Async XLA Ops:
  0.6 6.9 %copy-start = (f32[512,3072]{1,0:T(8,128)S(1)}, f32[512,3072]{1,0:T(8,128)}, u32[]{:S(2)}) copy-start(f32[512,3072]{1,0:T(8,128)} %stored.9) | copy-start | bytes 18874372
  0.6 8.6 %copy-start.9 = (f32[64,3072]{1,0:T(8,128)S(1)}, f32[64,3072]{1,0:T(8,128)}, u32[]{:S(2)}) copy-start(f32[64,3072]{1,0:T(8,128)} %refs_0_.1) | copy-start | bytes 2359300
  11.8 13.7 %copy-start.14 = (s32[24,7]{0,1:T(8,128)S(1)}, s32[24,7]{0,1:T(8,128)}, u32[]{:S(2)}) copy-start(s32[24,7]{0,1:T(8,128)} %param.6) | copy-start | bytes 2020
  11.8 13.9 %copy-start.15 = (s32[24]{0:T(128)S(1)}, s32[24]{0:T(128)}, u32[]{:S(2)}) copy-start(s32[24]{0:T(128)} %param.7) | copy-start | bytes 292
  14.0 29.0 %all-to-all-start = ((f32[128,1,1792]{2,1,0:T(1,128)}), f32[128,1,1792]{2,1,0:T(1,128)S(1)}, u32[]{:S(2)}, u32[]{:S(2)}) async-start(f32[128,1,1792]{2,1,0:T(1,128)} %copy.27), calls=%async_computation | async-start | bytes 1835008 | tf_op jit(solution)/shard_map/all_to_all | solution.py:39
  45.0 22.0 %all-to-all-start.1 = ((f32[128,1,1792]{2,1,0:T(1,128)}), f32[128,1,1792]{2,1,0:T(1,128)S(1)}, u32[]{:S(2)}, u32[]{:S(2)}) async-start(f32[128,1,1792]{2,1,0:T(1,128)} %broadcast_in_dim.80), calls=%async_computation.1 | async-start | bytes 1835008 | tf_op jit(solution)/shard_map/all_to_all | solution.py:41
  67.1 2.6 %slice-start = ((s8[6291456]{0:T(1024)(128)(4,1)}), s8[4194304]{0:T(1024)(128)(4,1)S(1)}, s32[]{:S(2)}) async-start(s8[6291456]{0:T(1024)(128)(4,1)} %bitcast.17), calls=%async_computation.6 | async-start | bytes 8388608
  67.1 3.2 %slice-start.1 = ((s8[6291456]{0:T(1024)(128)(4,1)}), s8[2097152]{0:T(1024)(128)(4,1)S(1)}, s32[]{:S(2)}) async-start(s8[6291456]{0:T(1024)(128)(4,1)} %bitcast.17), calls=%async_computation.7 | async-start | bytes 4194304
  67.9 4.6 %copy-start.4 = (f32[512,512]{1,0:T(8,128)}, f32[512,512]{1,0:T(8,128)S(1)}, u32[]{:S(2)}) copy-start(f32[512,512]{1,0:T(8,128)S(1)} %get-tuple-element.28.s) | copy-start | bytes 3145732
  72.5 24.9 %slice-start.2 = ((s8[6291456]{0:T(1024)(128)(4,1)}), s8[2097152]{0:T(1024)(128)(4,1)S(1)}, s32[]{:S(2)}) async-start(s8[6291456]{0:T(1024)(128)(4,1)} %bitcast.19), calls=%async_computation.8 | async-start | bytes 4194304
  72.5 24.9 %collective-permute-start = (f32[64,3072]{1,0:T(8,128)S(1)}, f32[64,3072]{1,0:T(8,128)}, u32[]{:S(2)}, u32[]{:S(2)}) collective-permute-start(f32[64,3072]{1,0:T(8,128)S(1)} %project.3.mid.prev.refs_1_.refs_2_), channel_id=1, source_target_pairs={{0,1},{1,2},{2,3},{3,4},{4,5},{5,6},{6,7},{7,8},{8,9},{9,10},{10,1... | collective-permute-start | bytes 2359304 | tf_op jit(solution)/shard_map/ppermute | solution.py:372
  73.0 24.4 %collective-permute-start.1 = (f32[64,3072]{1,0:T(8,128)S(1)}, f32[64,3072]{1,0:T(8,128)}, u32[]{:S(2)}, u32[]{:S(2)}) collective-permute-start(f32[64,3072]{1,0:T(8,128)S(1)} %project.3.mid.prev.refs_1_.refs_2_), channel_id=1, source_target_pairs={{1,0},{2,1},{3,2},{4,3},{5,4},{6,5},{7,6},{8,7},{9,8},{10,9},{11,1... | collective-permute-start | bytes 2359304 | tf_op jit(solution)/shard_map/ppermute | solution.py:372
  83.7 4.1 %copy-start.1 = (f32[24,7,128,128]{3,2,1,0:T(8,128)S(1)}, f32[24,7,128,128]{3,2,1,0:T(8,128)}, u32[]{:S(2)}) copy-start(f32[24,7,128,128]{3,2,1,0:T(8,128)} %param.5) | copy-start | bytes 33030148
  87.8 9.7 %slice-start.3 = ((s8[6291456]{0:T(1024)(128)(4,1)}), s8[4194304]{0:T(1024)(128)(4,1)S(1)}, s32[]{:S(2)}) async-start(s8[6291456]{0:T(1024)(128)(4,1)} %bitcast.19), calls=%async_computation.9 | async-start | bytes 8388608
  107.6 0.9 copy-start.12
  129.2 15.3 %all-to-all-start.3 = ((f32[128,1,384]{2,1,0:T(1,128)}), f32[128,1,384]{2,1,0:T(1,128)}, u32[]{:S(2)}, u32[]{:S(2)}) async-start(f32[128,1,384]{2,1,0:T(1,128)} %broadcast_in_dim.81), calls=%async_computation.3 | async-start | bytes 393216 | tf_op jit(solution)/shard_map/all_to_all | solution.py:41
  134.0 1.2 copy-start.5
  135.3 16.0 %slice-start.4 = ((s8[6291456]{0:T(1024)(128)(4,1)}), s8[2097152]{0:T(1024)(128)(4,1)S(1)}, s32[]{:S(2)}) async-start(s8[6291456]{0:T(1024)(128)(4,1)} %bitcast.21), calls=%async_computation.10 | async-start | bytes 4194304
  145.4 15.6 %slice-start.8 = ((s8[11010048]{0:T(1024)(128)(4,1)}), s8[4194304]{0:T(1024)(128)(4,1)S(1)}, s32[]{:S(2)}) async-start(s8[11010048]{0:T(1024)(128)(4,1)} %bitcast.26), calls=%async_computation.14 | async-start | bytes 8388608
  145.4 1.4 copy-start.6
  146.8 4.4 %slice-start.5 = ((s8[6291456]{0:T(1024)(128)(4,1)}), s8[4194304]{0:T(1024)(128)(4,1)S(1)}, s32[]{:S(2)}) async-start(s8[6291456]{0:T(1024)(128)(4,1)} %bitcast.21), calls=%async_computation.11 | async-start | bytes 8388608
  146.8 4.4 %copy-start.13 = (f32[64,3072]{1,0:T(8,128)S(1)}, f32[64,3072]{1,0:T(8,128)}, u32[]{:S(2)}) copy-start(f32[64,3072]{1,0:T(8,128)} %copy-done.12) | copy-start | bytes 2359300
  146.8 14.2 %slice-start.9 = ((s8[11010048]{0:T(1024)(128)(4,1)}), s8[4194304]{0:T(1024)(128)(4,1)S(1)}, s32[]{:S(2)}) async-start(s8[11010048]{0:T(1024)(128)(4,1)} %bitcast.26), calls=%async_computation.15 | async-start | bytes 8388608
  146.8 14.2 %slice-start.10 = ((s8[11010048]{0:T(1024)(128)(4,1)}), s8[2621440]{0:T(1024)(128)(4,1)S(1)}, s32[]{:S(2)}) async-start(s8[11010048]{0:T(1024)(128)(4,1)} %bitcast.26), calls=%async_computation.16 | async-start | bytes 5242880
  153.5 34.5 %copy-start.2 = (f32[64,3072]{1,0:T(8,128)}, f32[64,3072]{1,0:T(8,128)S(1)}, u32[]{:S(2)}) copy-start(f32[64,3072]{1,0:T(8,128)S(1)} %project.4.mid.refs_1_) | copy-start | bytes 2359300
  153.5 25.2 %collective-permute-start.2 = (f32[64,3072]{1,0:T(8,128)S(1)}, f32[64,3072]{1,0:T(8,128)S(1)}, u32[]{:S(2)}, u32[]{:S(2)}) collective-permute-start(f32[64,3072]{1,0:T(8,128)S(1)} %project.4.mid.refs_1_), channel_id=1, source_target_pairs={{0,1},{1,2},{2,3},{3,4},{4,5},{5,6},{6,7},{7,8},{8,9},{9,10},{10,1... | collective-permute-start | bytes 2359304 | tf_op jit(solution)/shard_map/ppermute | solution.py:372
  153.9 24.8 %collective-permute-start.3 = (f32[64,3072]{1,0:T(8,128)S(1)}, f32[64,3072]{1,0:T(8,128)S(1)}, u32[]{:S(2)}, u32[]{:S(2)}) collective-permute-start(f32[64,3072]{1,0:T(8,128)S(1)} %project.4.mid.refs_1_), channel_id=1, source_target_pairs={{1,0},{2,1},{3,2},{4,3},{5,4},{6,5},{7,6},{8,7},{9,8},{10,9},{11,1... | collective-permute-start | bytes 2359304 | tf_op jit(solution)/shard_map/ppermute | solution.py:372
  188.0 0.9 copy-start.10
  209.1 28.2 %slice-start.6 = ((s8[6291456]{0:T(1024)(128)(4,1)}), s8[2097152]{0:T(1024)(128)(4,1)S(1)}, s32[]{:S(2)}) async-start(s8[6291456]{0:T(1024)(128)(4,1)} %bitcast.23), calls=%async_computation.12 | async-start | bytes 4194304
  209.1 15.4 %all-to-all-start.5 = ((f32[128,1,384]{2,1,0:T(1,128)}), f32[128,1,384]{2,1,0:T(1,128)}, u32[]{:S(2)}, u32[]{:S(2)}) async-start(f32[128,1,384]{2,1,0:T(1,128)} %broadcast_in_dim.82), calls=%async_computation.5 | async-start | bytes 393216 | tf_op jit(solution)/shard_map/all_to_all | solution.py:41
  214.1 1.2 copy-start.7
  225.5 1.2 copy-start.8
  226.7 10.6 %slice-start.7 = ((s8[6291456]{0:T(1024)(128)(4,1)}), s8[4194304]{0:T(1024)(128)(4,1)S(1)}, s32[]{:S(2)}) async-start(s8[6291456]{0:T(1024)(128)(4,1)} %bitcast.23), calls=%async_computation.13 | async-start | bytes 8388608
  226.7 10.6 %copy-start.3 = (f32[64,3072]{1,0:T(8,128)S(1)}, f32[64,3072]{1,0:T(8,128)}, u32[]{:S(2)}) copy-start(f32[64,3072]{1,0:T(8,128)} %copy-done.2) | copy-start | bytes 2359300
  226.7 10.6 %copy-start.11 = (f32[64,3072]{1,0:T(8,128)S(1)}, f32[64,3072]{1,0:T(8,128)}, u32[]{:S(2)}) copy-start(f32[64,3072]{1,0:T(8,128)} %copy-done.10) | copy-start | bytes 2359300

commit v3 on v2

--- a/solution.py
+++ b/solution.py
@@ -14,8 +14,8 @@
 F32 = jnp.float32
 BF16 = jnp.bfloat16
 RB = 4
-CHUNK = 4
-TILE = 512
+CHUNK = 8
+TILE = 1024
 VMEM_LIMIT = 12 * 1024 * 1024
 
 
@@ -241,20 +241,22 @@
     lane = lax.broadcasted_iota(jnp.int32, (n, 2 * n), 1)
     eye = (lane == row + n).astype(F32)
     m = jnp.where(lane < n, jnp.concatenate([gram, gram], axis=1), eye)
-    scale = jnp.zeros((n, 2 * n), F32)
+    pivots = jnp.ones((n, 2 * n), F32)
     for p in range(0, n, PANEL):
         cols = [jnp.broadcast_to(m[:, p + j : p + j + 1], (n, 2 * n)) for j in range(PANEL)]
         for j in range(PANEL):
             k = p + j
             pivot = cols[j][k : k + 1]
-            root = lax.rsqrt(pivot)
-            root = root * (1.5 - 0.5 * pivot * root * root)
-            f = jnp.where(row > k, cols[j] * (root * root), 0.0)
-            scale = jnp.where(row == k, root, scale)
-            m = m - f * m[k : k + 1]
+            inv = pl.reciprocal(pivot, approx=True)
+            inv = inv * (2.0 - pivot * inv)
+            inv = inv * (2.0 - pivot * inv)
+            pivots = jnp.where(row == k, pivot, pivots)
+            f = jnp.where(row > k, cols[j], 0.0) * inv
             for q in range(j + 1, PANEL):
                 cols[q] = cols[q] - f * cols[q][k : k + 1]
-    m = m * scale
+            m = m - f * m[k : k + 1]
+    root = lax.rsqrt(pivots)
+    m = m * (root * (1.5 - 0.5 * pivots * root * root))
     upper = jnp.where(lane >= row, m, 0.0)[:, :n]
     return upper, m[:, n:]
 
@@ -267,17 +269,19 @@
     return mst, a[:, :bw], a[:, bw:], b[:, :bw], b[:, bw:]
 
 
-def first_kernel(t, s, c1t_out, minus_dt):
+def first_kernel(packed, s, c1t_out, minus_dt):
     bw, ks = c1t_out.shape
-    half = ks // 2
-    packed = t[...]
-    cut = packed.shape[1] // 2
-    packed = jnp.concatenate([packed[:, :cut], packed[:, cut:]], axis=0)
-    s12 = packed[:, half : 2 * half]
-    s[:half] = packed[:, : 2 * half]
-    s[half:] = jnp.concatenate([s12.T, packed[:, 2 * half : 3 * half]], axis=1)
-    t = packed[:, 3 * half :].T
-    c1t = jnp.concatenate([t[:bw], t[bw:]], axis=1)
+    cut = ks // 4
+    at = 0
+    for q in range(4):
+        for k in range(q, 4):
+            block = packed[:, at : at + cut]
+            at += cut
+            s[q * cut : (q + 1) * cut, k * cut : (k + 1) * cut] = block
+            if k > q:
+                s[k * cut : (k + 1) * cut, q * cut : (q + 1) * cut] = block.T
+    t = packed[:, at:].T
+    c1t = jnp.concatenate([t[q * bw : (q + 1) * bw] for q in range(4)], axis=1)
     c1t_out[...] = c1t
     minus_dt[...] = dot_nn(c1t, s[...]) - 2.0 * c1t
 
@@ -371,13 +375,13 @@
     def halo(w):
         return lax.ppermute(w, AXES, up), lax.ppermute(w, AXES, down)
 
-    half = ks // 2
-    top = dot_nt(stored[:half], stored, HIGH)
-    corner = dot_nt(stored[half:], stored[half:], HIGH)
+    half, cut = ks // 2, ks // 4
+    upper, lower = stored[:half], stored[half:]
+    s11, s12, s22 = dot_nt(upper, upper, HIGH), dot_nt(upper, lower, HIGH), dot_nt(lower, lower, HIGH)
     first = dot_nt(stored, start_block, HIGH)
-    packed = jnp.concatenate([top, corner, first[:half], first[half:]], axis=1)
-    packed = jnp.concatenate([packed[:devices], packed[devices:]], axis=1)
-    packed = total(packed[:, None, :])
+    packed = [s11[:cut], s12[:cut], s11[cut:, cut:], s12[cut:], s22[:cut], s22[cut:, cut:]]
+    packed += [first[q * cut : (q + 1) * cut] for q in range(4)]
+    packed = total(jnp.concatenate(packed, axis=1)[:, None])
     wide = (bw, ks)
     s, c1t, minus_dt = small(first_kernel, "first", [(ks, ks), wide, wide], packed)
     w1 = project(minus_dt, jnp.eye(bw, dtype=F32), stored, start_block)

time: 239 us -> 234 us (0.979)
  Pallas kernels: 58.9 us -> 50.9 us
    pallas_call x2, Pallas kernels: 19.4 us -> 14 us  [far_op(): pl.pallas_call(far_kernel, in_specs=[SMEM] + [VMEM] * 8, out_specs=[VMEM]...]
    dot_general x3 -> x4, matrix products: 11.1 us -> 13.3 us  [dot_nt(): lax.dot_general(a, b, (((1,), (1,)), ((), ())), precision=precision, pref...]
    unnamed x57 -> x66, local copies, waits for them, and re-layouts: 15.3 us -> 15.5 us
  transfers between devices with their start and end apart: 8 -> 8, of which waited for: 6 -> 6; matrix products, arithmetic and copies ran while one was open for 1% -> 1% of each run, Pallas kernels for 7% -> 6%
where the time goes in v3:
time: 234 us
  waiting for transfers between devices  63.1 us (27%)
  Pallas kernels  50.9 us (22%)
  starting transfers between devices  41 us (18%)
  blocking collectives  39 us (17%)
  local copies, waits for them, and re-layouts  20.5 us (9%)
  matrix products  13.3 us (6%)
  other arithmetic  3.4 us (1%)
  between operations  2.5 us (1%)
    all_to_all x2, blocking collectives, total(): parts = lax.all_to_all(x, AXES, 0, 0, tiled=True)  39 us
    all_to_all x3, waiting for transfers between devices, total(): lax.all_to_all(jnp.broadcast_to(mine, x.shape), AXES, 0, 0, tiled=True)  32.6 us
    pallas_call x5, Pallas kernels, small(): pl.pallas_call(kernel, out_shape=[jax.ShapeDtypeStruct(s, F32) for s in s...  17.9 us
    all_to_all x1, waiting for transfers between devices, total(): parts = lax.all_to_all(x, AXES, 0, 0, tiled=True)  15.8 us
    unnamed x66, local copies, waits for them, and re-layouts  15.5 us
    ppermute x4, starting transfers between devices, halo(): return (lax.ppermute(w, AXES, up), lax.ppermute(w, AXES, down))  15.1 us
    ppermute x4, waiting for transfers between devices, halo(): return (lax.ppermute(w, AXES, up), lax.ppermute(w, AXES, down))  14.8 us
    all_to_all x3, starting transfers between devices, total(): lax.all_to_all(jnp.broadcast_to(mine, x.shape), AXES, 0, 0, tiled=True)  14.4 us
  transfers between devices with their start and end apart: 8, of which 6 were waited for; matrix products, arithmetic and copies ran while one was open for 1% of the time, Pallas kernels for 6%

profile of v3, /device:TPU:1, one launch (start us, length us, event | category | flops | bytes accessed | tf_op | source)
XLA Modules:
  0.0 233.8 jit_solution(7973873374015219076)
XLA Ops:
  0.6 4.4 %fusion.5 = f32[256,256]{0,1:T(8,128)S(1)} fusion(f32[512,3072]{1,0:T(8,128)} %stored.9), kind=kOutput, calls=%fused_computation.5 | convolution fusion | flops 1207959552 | bytes 3407872 | tf_op jit(solution)/shard_map/dot_general | solution.py:23
  5.1 4.3 %fusion.2 = f32[256,256]{0,1:T(8,128)S(1)} fusion(f32[512,3072]{1,0:T(8,128)} %stored.9), kind=kOutput, calls=%fused_computation.2 | convolution fusion | flops 1207959552 | bytes 6553600 | tf_op jit(solution)/shard_map/dot_general | solution.py:23
  9.4 1.6 fusion
  11.1 3.0 %fusion.13 = f32[512,64]{0,1:T(8,128)S(1)} fusion(f32[512,3072]{1,0:T(8,128)S(1)} %copy-done, f32[64,3072]{1,0:T(8,128)S(1)} %copy-done.9), kind=kOutput, calls=%fused_computation.50 | convolution fusion | flops 603979776 | bytes 7208960 | tf_op jit(solution)/shard_map/dot_general | solution.py:23
  14.2 1.7 copy.15
  15.9 11.5 %all-to-all-start = ((f32[128,1,1536]{2,1,0:T(1,128)}), f32[128,1,1536]{2,1,0:T(1,128)S(1)}, u32[]{:S(2)}, u32[]{:S(2)}) async-start(f32[128,1,1536]{2,1,0:T(1,128)} %copy.15), calls=%async_computation | async-start | bytes 1572864 | tf_op jit(solution)/shard_map/all_to_all | solution.py:39
  27.5 0.1 copy.14
  27.6 0.1 reshape.83
  27.7 0.1 copy.13
  27.8 0.1 lt.113
  27.9 15.8 %all-to-all-done = f32[128,1,1536]{2,1,0:T(1,128)S(1)} async-done(((f32[128,1,1536]{2,1,0:T(1,128)}), f32[128,1,1536]{2,1,0:T(1,128)S(1)}, u32[]{:S(2)}, u32[]{:S(2)}) %all-to-all-start) | async-done | bytes 786464 | tf_op jit(solution)/shard_map/all_to_all | solution.py:39
  43.7 0.5 reduce_sum.107
  44.2 1.3 broadcast_in_dim.80
  45.5 4.3 %all-to-all-start.1 = ((f32[128,1,1536]{2,1,0:T(1,128)}), f32[128,1,1536]{2,1,0:T(1,128)S(1)}, u32[]{:S(2)}, u32[]{:S(2)}) async-start(f32[128,1,1536]{2,1,0:T(1,128)} %broadcast_in_dim.80), calls=%async_computation.1 | async-start | bytes 1572864 | tf_op jit(solution)/shard_map/all_to_all | solution.py:41
  49.8 0.1 convert_reduce_fusion
  49.9 0.1 convert_reduce_fusion.1
  50.1 0.2 select_reduce_fusion
  50.2 15.8 %all-to-all-done.1 = f32[128,1,1536]{2,1,0:T(1,128)S(1)} async-done(((f32[128,1,1536]{2,1,0:T(1,128)}), f32[128,1,1536]{2,1,0:T(1,128)S(1)}, u32[]{:S(2)}, u32[]{:S(2)}) %all-to-all-start.1) | async-done | bytes 786464 | tf_op jit(solution)/shard_map/all_to_all | solution.py:41
  66.1 0.1 copy.22
  66.1 0.0 slice-start.1
  66.1 0.7 first.1
  66.9 1.8 slice-done
  68.6 0.7 slice-done.1
  69.3 1.8 project.3.mid.prev.refs_1_.refs_2_
  71.2 0.0 slice-start.2
  71.2 0.5 collective-permute-start
  71.6 7.1 %collective-permute-start.1 = (f32[64,3072]{1,0:T(8,128)S(1)}, f32[64,3072]{1,0:T(8,128)}, u32[]{:S(2)}, u32[]{:S(2)}) collective-permute-start(f32[64,3072]{1,0:T(8,128)S(1)} %project.3.mid.prev.refs_1_.refs_2_), channel_id=1, source_target_pairs={{1,0},{2,1},{3,2},{4,3},{5,4},{6,5},{7,6},{8,7},{9,8},{10,9},{11,1... | collective-permute-start | bytes 2359304 | tf_op jit(solution)/shard_map/ppermute | solution.py:376
  78.7 0.6 convert_reduce_fusion.2
  80.7 0.2 select_reduce_fusion.2
  80.9 1.3 compare_select_fusion.1
  82.2 0.1 concatenate.6.plan
  82.3 4.1 %copy-done.1 = f32[24,7,128,128]{3,2,1,0:T(8,128)S(1)} copy-done((f32[24,7,128,128]{3,2,1,0:T(8,128)S(1)}, f32[24,7,128,128]{3,2,1,0:T(8,128)}, u32[]{:S(2)}) %copy-start.1) | copy-done | bytes 11010072
  86.4 6.2 %near_op.2 = (f32[24,128,128]{2,1,0:T(8,128)S(1)}, bf16[168,128,256]{2,1,0:T(8,128)(2,1)S(1)}, f32[64,64]{1,0:T(8,128)S(1)}) custom-call(s32[1014]{0:T(1024)S(1)} %concatenate.6.plan, f32[168,128,128]{2,1,0:T(8,128)S(1)} %bitcast.23, f32[64,3072]{1,0:T(8,128)S(1)} %project.3.mid.prev.refs_1_.refs_2_), custom_call_target="tpu_custom_call" | custom-call | flops 2000000000 | bytes 12582912 | tf_op jit(solution)/shard_map/near_op/pallas_call | solution.py:144
  92.6 3.3 %collective-permute-done.left = f32[64,3072]{1,0:T(8,128)} collective-permute-done((f32[64,3072]{1,0:T(8,128)S(1)}, f32[64,3072]{1,0:T(8,128)}, u32[]{:S(2)}, u32[]{:S(2)}) %collective-permute-start) | collective-permute-done | bytes 786464 | tf_op jit(solution)/shard_map/ppermute | solution.py:376
  96.0 7.4 %far_op.2 = (f32[64,3072]{1,0:T(8,128)S(1)}, f32[128,1,384]{2,1,0:T(1,128)S(1)}) custom-call(s32[1014]{0:T(1024)S(1)} %concatenate.6.plan, bf16[168,128,256]{2,1,0:T(8,128)(2,1)S(1)} %get-tuple-element.24.halves, f32[512,3072]{1,0:T(8,128)S(1)} %bitcast.18, f32[64,3072]{1,0:T(8,128)} %collective-permute-done.left, f32[64,3072]{1,0:T(8,128)} %collective-permute-done.1.right, ...), custom_call_target="tpu_custom_call" | custom-call | flops 2000000000 | bytes 20971520 | tf_op jit(solution)/shard_map/far_op/pallas_call | solution.py:164
  103.4 0.9 copy-done.12
  104.3 19.8 %all_to_all.30 = f32[128,1,384]{2,1,0:T(1,128)S(1)} all-to-all(f32[128,1,384]{2,1,0:T(1,128)S(1)} %get-tuple-element.27), channel_id=1, replica_groups=mesh['row'=4,'basis'=8,'rep'=4] {'row','basis','rep'}, dimensions={0} | all-to-all | bytes 393216 | tf_op jit(solution)/shard_map/all_to_all | solution.py:39
  124.1 0.2 reduce_sum.108
  124.2 0.8 broadcast_in_dim.81
  125.0 4.8 %all-to-all-start.3 = ((f32[128,1,384]{2,1,0:T(1,128)}), f32[128,1,384]{2,1,0:T(1,128)}, u32[]{:S(2)}, u32[]{:S(2)}) async-start(f32[128,1,384]{2,1,0:T(1,128)} %broadcast_in_dim.81), calls=%async_computation.3 | async-start | bytes 393216 | tf_op jit(solution)/shard_map/all_to_all | solution.py:41
  129.9 1.2 copy-done.5
  131.1 0.7 after_first.1.c3t
  131.8 8.5 %all-to-all-done.3 = f32[128,1,384]{2,1,0:T(1,128)} async-done(((f32[128,1,384]{2,1,0:T(1,128)}), f32[128,1,384]{2,1,0:T(1,128)}, u32[]{:S(2)}, u32[]{:S(2)}) %all-to-all-start.3) | async-done | bytes 196640 | tf_op jit(solution)/shard_map/all_to_all | solution.py:41
  140.3 0.9 copy.24
  141.2 1.4 copy-done.6
  142.6 4.6 %second.1 = (f32[64,512]{1,0:T(8,128)S(1)}, f32[64,128]{1,0:T(8,128)S(1)}, f32[192,512]{1,0:T(8,128)S(1)}) custom-call(f32[128,384]{1,0:T(8,128)S(1)} %bitcast.29, f32[512,512]{1,0:T(8,128)S(1)} %copy-done.6, f32[64,512]{1,0:T(8,128)S(1)} %after_first.1.c3t), custom_call_target="tpu_custom_call" | custom-call | flops 10000000000 | bytes 2097152 | tf_op jit(solution)/shard_map/second/pallas_call | solution.py:352
  147.2 1.9 project.4.mid.refs_1_
  149.1 0.4 collective-permute-start.2
  149.5 7.2 %collective-permute-start.3 = (f32[64,3072]{1,0:T(8,128)S(1)}, f32[64,3072]{1,0:T(8,128)S(1)}, u32[]{:S(2)}, u32[]{:S(2)}) collective-permute-start(f32[64,3072]{1,0:T(8,128)S(1)} %project.4.mid.refs_1_), channel_id=1, source_target_pairs={{1,0},{2,1},{3,2},{4,3},{5,4},{6,5},{7,6},{8,7},{9,8},{10,9},{11,1... | collective-permute-start | bytes 2359304 | tf_op jit(solution)/shard_map/ppermute | solution.py:376
  156.7 6.2 %near_op.3 = (f32[24,128,128]{2,1,0:T(8,128)S(1)}, bf16[168,128,256]{2,1,0:T(8,128)(2,1)S(1)}, f32[64,64]{1,0:T(8,128)S(1)}) custom-call(s32[1014]{0:T(1024)S(1)} %concatenate.6.plan, f32[168,128,128]{2,1,0:T(8,128)S(1)} %bitcast.26, f32[64,3072]{1,0:T(8,128)S(1)} %project.4.mid.refs_1_), custom_call_target="tpu_custom_call" | custom-call | flops 2000000000 | bytes 12582912 | tf_op jit(solution)/shard_map/near_op/pallas_call | solution.py:144
  162.9 11.4 %collective-permute-done.2.left = f32[64,3072]{1,0:T(8,128)S(1)} collective-permute-done((f32[64,3072]{1,0:T(8,128)S(1)}, f32[64,3072]{1,0:T(8,128)S(1)}, u32[]{:S(2)}, u32[]{:S(2)}) %collective-permute-start.2) | collective-permute-done | bytes 786464 | tf_op jit(solution)/shard_map/ppermute | solution.py:376
  174.3 6.6 %far_op.3 = (f32[64,3072]{1,0:T(8,128)S(1)}, f32[128,1,384]{2,1,0:T(1,128)S(1)}) custom-call(s32[1014]{0:T(1024)S(1)} %concatenate.6.plan, bf16[168,128,256]{2,1,0:T(8,128)(2,1)S(1)} %get-tuple-element.33.halves, f32[512,3072]{1,0:T(8,128)S(1)} %bitcast.20, f32[64,3072]{1,0:T(8,128)S(1)} %collective-permute-done.2.left, ...), custom_call_target="tpu_custom_call" | custom-call | flops 2000000000 | bytes 20971520 | tf_op jit(solution)/shard_map/far_op/pallas_call | solution.py:164
  181.0 0.9 copy-done.10
  181.8 19.3 %all_to_all.31 = f32[128,1,384]{2,1,0:T(1,128)S(1)} all-to-all(f32[128,1,384]{2,1,0:T(1,128)S(1)} %get-tuple-element.36), channel_id=1, replica_groups=mesh['row'=4,'basis'=8,'rep'=4] {'row','basis','rep'}, dimensions={0} | all-to-all | bytes 393216 | tf_op jit(solution)/shard_map/all_to_all | solution.py:39
  201.1 0.2 reduce_sum.109
  201.3 0.8 broadcast_in_dim.82
  202.0 5.2 %all-to-all-start.5 = ((f32[128,1,384]{2,1,0:T(1,128)}), f32[128,1,384]{2,1,0:T(1,128)}, u32[]{:S(2)}, u32[]{:S(2)}) async-start(f32[128,1,384]{2,1,0:T(1,128)} %broadcast_in_dim.82), calls=%async_computation.5 | async-start | bytes 393216 | tf_op jit(solution)/shard_map/all_to_all | solution.py:41
  207.3 1.2 copy-done.7
  208.5 0.9 after.1.c3
  209.4 8.3 %all-to-all-done.5 = f32[128,1,384]{2,1,0:T(1,128)} async-done(((f32[128,1,384]{2,1,0:T(1,128)}), f32[128,1,384]{2,1,0:T(1,128)}, u32[]{:S(2)}, u32[]{:S(2)}) %all-to-all-start.5) | async-done | bytes 196640 | tf_op jit(solution)/shard_map/all_to_all | solution.py:41
  217.7 0.9 copy.23
  218.7 1.2 copy-done.8
  219.9 11.0 %third.1 = (f32[64,512]{1,0:T(8,128)S(1)}, f32[64,192]{1,0:T(8,128)S(1)}, f32[2,64,64]{2,1,0:T(8,128)}, f32[2,64,64]{2,1,0:T(8,128)}) custom-call(f32[128,384]{1,0:T(8,128)S(1)} %bitcast.28, f32[512,512]{1,0:T(8,128)S(1)} %copy-done.8, f32[64,640]{1,0:T(8,128)S(1)} %after.1.c3, f32[192,512]{1,0:T(8,128)S(1)} %get-tuple-element.37.keep), custom_call_target="tpu_custom_call" | custom-call | flops 10000000000 | bytes 2097152 | tf_op jit(solution)/shard_map/third/pallas_call | solution.py:352
  230.9 2.9 %project.5 = f32[64,3072]{1,0:T(8,128)} custom-call(f32[64,512]{1,0:T(8,128)S(1)} %get-tuple-element.40.cs, f32[64,192]{1,0:T(8,128)S(1)} %get-tuple-element.41.cw, f32[512,3072]{1,0:T(8,128)S(1)} %bitcast.22, f32[64,3072]{1,0:T(8,128)S(1)} %copy-done.11, f32[64,3072]{1,0:T(8,128)S(1)} %copy-done.3, f32[64,3072]{1,0:T(8,128)S(1)} %project.3.mid.prev.refs_1_.refs_2_), custom_call_target="tpu_custom_call" | custom-call | tf_op jit(solution)/shard_map/project/pallas_call | solution.py:225
  (66 shorter events, 0.3 us)
Async XLA Ops:
  0.6 8.8 %copy-start = (f32[512,3072]{1,0:T(8,128)S(1)}, f32[512,3072]{1,0:T(8,128)}, u32[]{:S(2)}) copy-start(f32[512,3072]{1,0:T(8,128)} %stored.9) | copy-start | bytes 18874372
  5.1 6.1 %copy-start.9 = (f32[64,3072]{1,0:T(8,128)S(1)}, f32[64,3072]{1,0:T(8,128)}, u32[]{:S(2)}) copy-start(f32[64,3072]{1,0:T(8,128)} %refs_0_.1) | copy-start | bytes 2359300
  11.0 16.4 %copy-start.14 = (s32[24,7]{0,1:T(8,128)S(1)}, s32[24,7]{0,1:T(8,128)}, u32[]{:S(2)}) copy-start(s32[24,7]{0,1:T(8,128)} %param.6) | copy-start | bytes 2020
  11.0 16.6 %copy-start.15 = (s32[24]{0:T(128)S(1)}, s32[24]{0:T(128)}, u32[]{:S(2)}) copy-start(s32[24]{0:T(128)} %param.7) | copy-start | bytes 292
  15.9 27.8 %all-to-all-start = ((f32[128,1,1536]{2,1,0:T(1,128)}), f32[128,1,1536]{2,1,0:T(1,128)S(1)}, u32[]{:S(2)}, u32[]{:S(2)}) async-start(f32[128,1,1536]{2,1,0:T(1,128)} %copy.15), calls=%async_computation | async-start | bytes 1572864 | tf_op jit(solution)/shard_map/all_to_all | solution.py:39
  45.5 20.6 %all-to-all-start.1 = ((f32[128,1,1536]{2,1,0:T(1,128)}), f32[128,1,1536]{2,1,0:T(1,128)S(1)}, u32[]{:S(2)}, u32[]{:S(2)}) async-start(f32[128,1,1536]{2,1,0:T(1,128)} %broadcast_in_dim.80), calls=%async_computation.1 | async-start | bytes 1572864 | tf_op jit(solution)/shard_map/all_to_all | solution.py:41
  66.1 2.6 %slice-start = ((s8[6291456]{0:T(1024)(128)(4,1)}), s8[4194304]{0:T(1024)(128)(4,1)S(1)}, s32[]{:S(2)}) async-start(s8[6291456]{0:T(1024)(128)(4,1)} %bitcast.15), calls=%async_computation.6 | async-start | bytes 8388608
  66.1 3.2 %slice-start.1 = ((s8[6291456]{0:T(1024)(128)(4,1)}), s8[2097152]{0:T(1024)(128)(4,1)S(1)}, s32[]{:S(2)}) async-start(s8[6291456]{0:T(1024)(128)(4,1)} %bitcast.15), calls=%async_computation.7 | async-start | bytes 4194304
  66.9 4.3 %copy-start.4 = (f32[512,512]{1,0:T(8,128)}, f32[512,512]{1,0:T(8,128)S(1)}, u32[]{:S(2)}) copy-start(f32[512,512]{1,0:T(8,128)S(1)} %get-tuple-element.28.s) | copy-start | bytes 3145732
  71.2 24.8 %slice-start.2 = ((s8[6291456]{0:T(1024)(128)(4,1)}), s8[2097152]{0:T(1024)(128)(4,1)S(1)}, s32[]{:S(2)}) async-start(s8[6291456]{0:T(1024)(128)(4,1)} %bitcast.17), calls=%async_computation.8 | async-start | bytes 4194304
  71.2 24.8 %collective-permute-start = (f32[64,3072]{1,0:T(8,128)S(1)}, f32[64,3072]{1,0:T(8,128)}, u32[]{:S(2)}, u32[]{:S(2)}) collective-permute-start(f32[64,3072]{1,0:T(8,128)S(1)} %project.3.mid.prev.refs_1_.refs_2_), channel_id=1, source_target_pairs={{0,1},{1,2},{2,3},{3,4},{4,5},{5,6},{6,7},{7,8},{8,9},{9,10},{10,1... | collective-permute-start | bytes 2359304 | tf_op jit(solution)/shard_map/ppermute | solution.py:376
  71.6 24.4 %collective-permute-start.1 = (f32[64,3072]{1,0:T(8,128)S(1)}, f32[64,3072]{1,0:T(8,128)}, u32[]{:S(2)}, u32[]{:S(2)}) collective-permute-start(f32[64,3072]{1,0:T(8,128)S(1)} %project.3.mid.prev.refs_1_.refs_2_), channel_id=1, source_target_pairs={{1,0},{2,1},{3,2},{4,3},{5,4},{6,5},{7,6},{8,7},{9,8},{10,9},{11,1... | collective-permute-start | bytes 2359304 | tf_op jit(solution)/shard_map/ppermute | solution.py:376
  82.3 4.1 %copy-start.1 = (f32[24,7,128,128]{3,2,1,0:T(8,128)S(1)}, f32[24,7,128,128]{3,2,1,0:T(8,128)}, u32[]{:S(2)}) copy-start(f32[24,7,128,128]{3,2,1,0:T(8,128)} %param.5) | copy-start | bytes 33030148
  86.4 9.6 %slice-start.3 = ((s8[6291456]{0:T(1024)(128)(4,1)}), s8[4194304]{0:T(1024)(128)(4,1)S(1)}, s32[]{:S(2)}) async-start(s8[6291456]{0:T(1024)(128)(4,1)} %bitcast.17), calls=%async_computation.9 | async-start | bytes 8388608
  103.4 0.9 copy-start.12
  125.0 15.3 %all-to-all-start.3 = ((f32[128,1,384]{2,1,0:T(1,128)}), f32[128,1,384]{2,1,0:T(1,128)}, u32[]{:S(2)}, u32[]{:S(2)}) async-start(f32[128,1,384]{2,1,0:T(1,128)} %broadcast_in_dim.81), calls=%async_computation.3 | async-start | bytes 393216 | tf_op jit(solution)/shard_map/all_to_all | solution.py:41
  129.8 1.2 copy-start.5
  131.1 16.1 %slice-start.4 = ((s8[6291456]{0:T(1024)(128)(4,1)}), s8[2097152]{0:T(1024)(128)(4,1)S(1)}, s32[]{:S(2)}) async-start(s8[6291456]{0:T(1024)(128)(4,1)} %bitcast.19), calls=%async_computation.10 | async-start | bytes 4194304
  141.2 15.5 %slice-start.8 = ((s8[11010048]{0:T(1024)(128)(4,1)}), s8[4194304]{0:T(1024)(128)(4,1)S(1)}, s32[]{:S(2)}) async-start(s8[11010048]{0:T(1024)(128)(4,1)} %bitcast.24), calls=%async_computation.14 | async-start | bytes 8388608
  141.2 1.4 copy-start.6
  142.6 4.6 %slice-start.5 = ((s8[6291456]{0:T(1024)(128)(4,1)}), s8[4194304]{0:T(1024)(128)(4,1)S(1)}, s32[]{:S(2)}) async-start(s8[6291456]{0:T(1024)(128)(4,1)} %bitcast.19), calls=%async_computation.11 | async-start | bytes 8388608
  142.6 4.6 %copy-start.13 = (f32[64,3072]{1,0:T(8,128)S(1)}, f32[64,3072]{1,0:T(8,128)}, u32[]{:S(2)}) copy-start(f32[64,3072]{1,0:T(8,128)} %copy-done.12) | copy-start | bytes 2359300
  142.6 14.1 %slice-start.9 = ((s8[11010048]{0:T(1024)(128)(4,1)}), s8[4194304]{0:T(1024)(128)(4,1)S(1)}, s32[]{:S(2)}) async-start(s8[11010048]{0:T(1024)(128)(4,1)} %bitcast.24), calls=%async_computation.15 | async-start | bytes 8388608
  142.6 14.1 %slice-start.10 = ((s8[11010048]{0:T(1024)(128)(4,1)}), s8[2621440]{0:T(1024)(128)(4,1)S(1)}, s32[]{:S(2)}) async-start(s8[11010048]{0:T(1024)(128)(4,1)} %bitcast.24), calls=%async_computation.16 | async-start | bytes 5242880
  149.1 31.8 %copy-start.2 = (f32[64,3072]{1,0:T(8,128)}, f32[64,3072]{1,0:T(8,128)S(1)}, u32[]{:S(2)}) copy-start(f32[64,3072]{1,0:T(8,128)S(1)} %project.4.mid.refs_1_) | copy-start | bytes 2359300
  149.1 25.2 %collective-permute-start.2 = (f32[64,3072]{1,0:T(8,128)S(1)}, f32[64,3072]{1,0:T(8,128)S(1)}, u32[]{:S(2)}, u32[]{:S(2)}) collective-permute-start(f32[64,3072]{1,0:T(8,128)S(1)} %project.4.mid.refs_1_), channel_id=1, source_target_pairs={{0,1},{1,2},{2,3},{3,4},{4,5},{5,6},{6,7},{7,8},{8,9},{9,10},{10,1... | collective-permute-start | bytes 2359304 | tf_op jit(solution)/shard_map/ppermute | solution.py:376
  149.5 24.8 %collective-permute-start.3 = (f32[64,3072]{1,0:T(8,128)S(1)}, f32[64,3072]{1,0:T(8,128)S(1)}, u32[]{:S(2)}, u32[]{:S(2)}) collective-permute-start(f32[64,3072]{1,0:T(8,128)S(1)} %project.4.mid.refs_1_), channel_id=1, source_target_pairs={{1,0},{2,1},{3,2},{4,3},{5,4},{6,5},{7,6},{8,7},{9,8},{10,9},{11,1... | collective-permute-start | bytes 2359304 | tf_op jit(solution)/shard_map/ppermute | solution.py:376
  180.9 0.9 copy-start.10
  202.0 28.8 %slice-start.6 = ((s8[6291456]{0:T(1024)(128)(4,1)}), s8[2097152]{0:T(1024)(128)(4,1)S(1)}, s32[]{:S(2)}) async-start(s8[6291456]{0:T(1024)(128)(4,1)} %bitcast.21), calls=%async_computation.12 | async-start | bytes 4194304
  202.0 15.7 %all-to-all-start.5 = ((f32[128,1,384]{2,1,0:T(1,128)}), f32[128,1,384]{2,1,0:T(1,128)}, u32[]{:S(2)}, u32[]{:S(2)}) async-start(f32[128,1,384]{2,1,0:T(1,128)} %broadcast_in_dim.82), calls=%async_computation.5 | async-start | bytes 393216 | tf_op jit(solution)/shard_map/all_to_all | solution.py:41
  207.3 1.2 copy-start.7
  218.6 1.2 copy-start.8
  219.9 11.0 %slice-start.7 = ((s8[6291456]{0:T(1024)(128)(4,1)}), s8[4194304]{0:T(1024)(128)(4,1)S(1)}, s32[]{:S(2)}) async-start(s8[6291456]{0:T(1024)(128)(4,1)} %bitcast.21), calls=%async_computation.13 | async-start | bytes 8388608
  219.9 11.0 %copy-start.3 = (f32[64,3072]{1,0:T(8,128)S(1)}, f32[64,3072]{1,0:T(8,128)}, u32[]{:S(2)}) copy-start(f32[64,3072]{1,0:T(8,128)} %copy-done.2) | copy-start | bytes 2359300
  219.9 11.0 %copy-start.11 = (f32[64,3072]{1,0:T(8,128)S(1)}, f32[64,3072]{1,0:T(8,128)}, u32[]{:S(2)}) copy-start(f32[64,3072]{1,0:T(8,128)} %copy-done.10) | copy-start | bytes 2359300

commit v4 on v3

--- a/solution.py
+++ b/solution.py
@@ -232,7 +232,7 @@
     )(cs, cw, stored, *arrays)
 
 
-PANEL = 4
+PANEL = 16
 
 
 def factor_of(gram):
@@ -377,7 +377,8 @@
 
     half, cut = ks // 2, ks // 4
     upper, lower = stored[:half], stored[half:]
-    s11, s12, s22 = dot_nt(upper, upper, HIGH), dot_nt(upper, lower, HIGH), dot_nt(lower, lower, HIGH)
+    top, s22 = dot_nt(upper, stored, HIGH), dot_nt(lower, lower, HIGH)
+    s11, s12 = top[:, :half], top[:, half:]
     first = dot_nt(stored, start_block, HIGH)
     packed = [s11[:cut], s12[:cut], s11[cut:, cut:], s12[cut:], s22[:cut], s22[cut:, cut:]]
     packed += [first[q * cut : (q + 1) * cut] for q in range(4)]

time: 234 us -> 227 us (0.970)
  Pallas kernels: 50.9 us -> 46.7 us
  waiting for transfers between devices: 63.1 us -> 60.6 us
    pallas_call x5, Pallas kernels: 17.9 us -> 14.3 us  [small(): pl.pallas_call(kernel, out_shape=[jax.ShapeDtypeStruct(s, F32) for s in s...]
    pallas_call x2, Pallas kernels: 14 us -> 10.9 us  [far_op(): pl.pallas_call(far_kernel, in_specs=[SMEM] + [VMEM] * 8, out_specs=[VMEM]...]
    ppermute x4, waiting for transfers between devices: 14.8 us -> 12.3 us  [halo(): return (lax.ppermute(w, AXES, up), lax.ppermute(w, AXES, down))]
    pallas_call x2, Pallas kernels: 12.4 us -> 14.9 us  [near_op(): pl.pallas_call(near_kernel, in_specs=[SMEM, VMEM, VMEM], out_specs=[VMEM]...]
    dot_general x4 -> x3, matrix products: 13.3 us -> 11.1 us  [dot_nt(): lax.dot_general(a, b, (((1,), (1,)), ((), ())), precision=precision, pref...]
    unnamed x66 -> x57, local copies, waits for them, and re-layouts: 15.5 us -> 15.4 us
  transfers between devices with their start and end apart: 8 -> 8, of which waited for: 6 -> 6; matrix products, arithmetic and copies ran while one was open for 1% -> 1% of each run, Pallas kernels for 6% -> 7%
where the time goes in v4:
time: 227 us; the launch traced here: 224 us
  waiting for transfers between devices  60.6 us (27%)
  Pallas kernels  46.7 us (21%)
  starting transfers between devices  41 us (18%)
  blocking collectives  38.6 us (17%)
  local copies, waits for them, and re-layouts  20.6 us (9%)
  matrix products  11.1 us (5%)
  other arithmetic  3.4 us (1%)
  between operations  2.47 us (1%)
    all_to_all x2, blocking collectives, total(): parts = lax.all_to_all(x, AXES, 0, 0, tiled=True)  38.6 us
    all_to_all x3, waiting for transfers between devices, total(): lax.all_to_all(jnp.broadcast_to(mine, x.shape), AXES, 0, 0, tiled=True)  32.6 us
    all_to_all x1, waiting for transfers between devices, total(): parts = lax.all_to_all(x, AXES, 0, 0, tiled=True)  15.8 us
    unnamed x57, local copies, waits for them, and re-layouts  15.4 us
    ppermute x4, starting transfers between devices, halo(): return (lax.ppermute(w, AXES, up), lax.ppermute(w, AXES, down))  15.1 us
    pallas_call x2, Pallas kernels, near_op(): pl.pallas_call(near_kernel, in_specs=[SMEM, VMEM, VMEM], out_specs=[VMEM]...  14.9 us
    all_to_all x3, starting transfers between devices, total(): lax.all_to_all(jnp.broadcast_to(mine, x.shape), AXES, 0, 0, tiled=True)  14.4 us
    pallas_call x5, Pallas kernels, small(): pl.pallas_call(kernel, out_shape=[jax.ShapeDtypeStruct(s, F32) for s in s...  14.3 us
  transfers between devices with their start and end apart: 8, of which 6 were waited for; matrix products, arithmetic and copies ran while one was open for 1% of the time, Pallas kernels for 7%

profile of v4, /device:TPU:1, one launch (start us, length us, event | category | flops | bytes accessed | tf_op | source)
XLA Modules:
  0.0 224.5 jit_solution(11942216906528463068)
XLA Ops:
  0.7 6.8 %fusion.2 = f32[256,512]{1,0:T(8,128)S(1)} fusion(f32[512,3072]{1,0:T(8,128)} %stored.9), kind=kOutput, calls=%fused_computation.2 | convolution fusion | flops 2415919104 | bytes 9961472 | tf_op jit(solution)/shard_map/dot_general | solution.py:23
  7.6 1.7 fusion
  9.3 2.6 %fusion.11 = f32[512,64]{1,0:T(8,128)S(1)} fusion(f32[512,3072]{1,0:T(8,128)S(1)} %copy-done, f32[64,3072]{1,0:T(8,128)S(1)} %copy-done.9), kind=kOutput, calls=%fused_computation.38 | convolution fusion | flops 603979776 | bytes 7208960 | tf_op jit(solution)/shard_map/dot_general | solution.py:23
  12.0 0.1 concatenate.8
  12.1 1.7 copy.39
  13.8 11.5 %all-to-all-start = ((f32[128,1,1536]{2,1,0:T(1,128)}), f32[128,1,1536]{2,1,0:T(1,128)S(1)}, u32[]{:S(2)}, u32[]{:S(2)}) async-start(f32[128,1,1536]{2,1,0:T(1,128)} %copy.39), calls=%async_computation | async-start | bytes 1572864 | tf_op jit(solution)/shard_map/all_to_all | solution.py:39
  25.3 0.1 copy.32
  25.4 0.1 reshape.83
  25.5 0.1 copy.31
  25.6 0.1 lt.113
  25.8 15.8 %all-to-all-done = f32[128,1,1536]{2,1,0:T(1,128)S(1)} async-done(((f32[128,1,1536]{2,1,0:T(1,128)}), f32[128,1,1536]{2,1,0:T(1,128)S(1)}, u32[]{:S(2)}, u32[]{:S(2)}) %all-to-all-start) | async-done | bytes 786464 | tf_op jit(solution)/shard_map/all_to_all | solution.py:39
  41.5 0.5 reduce_sum.107
  42.0 1.3 broadcast_in_dim.80
  43.3 4.3 %all-to-all-start.1 = ((f32[128,1,1536]{2,1,0:T(1,128)}), f32[128,1,1536]{2,1,0:T(1,128)S(1)}, u32[]{:S(2)}, u32[]{:S(2)}) async-start(f32[128,1,1536]{2,1,0:T(1,128)} %broadcast_in_dim.80), calls=%async_computation.1 | async-start | bytes 1572864 | tf_op jit(solution)/shard_map/all_to_all | solution.py:41
  47.7 0.1 convert_reduce_fusion
  47.8 0.1 convert_reduce_fusion.1
  47.9 0.2 select_reduce_fusion
  48.1 15.8 %all-to-all-done.1 = f32[128,1,1536]{2,1,0:T(1,128)S(1)} async-done(((f32[128,1,1536]{2,1,0:T(1,128)}), f32[128,1,1536]{2,1,0:T(1,128)S(1)}, u32[]{:S(2)}, u32[]{:S(2)}) %all-to-all-start.1) | async-done | bytes 786464 | tf_op jit(solution)/shard_map/all_to_all | solution.py:41
  63.9 0.1 copy.48
  64.0 0.0 slice-start.1
  64.0 0.7 first.1
  64.7 1.8 slice-done
  66.5 0.7 slice-done.1
  67.2 1.8 project.3.mid.prev.refs_1_.refs_2_
  69.0 0.0 slice-start.2
  69.0 0.5 collective-permute-start
  69.5 7.1 %collective-permute-start.1 = (f32[64,3072]{1,0:T(8,128)S(1)}, f32[64,3072]{1,0:T(8,128)}, u32[]{:S(2)}, u32[]{:S(2)}) collective-permute-start(f32[64,3072]{1,0:T(8,128)S(1)} %project.3.mid.prev.refs_1_.refs_2_), channel_id=1, source_target_pairs={{1,0},{2,1},{3,2},{4,3},{5,4},{6,5},{7,6},{8,7},{9,8},{10,9},{11,1... | collective-permute-start | bytes 2359304 | tf_op jit(solution)/shard_map/ppermute | solution.py:376
  76.6 0.6 convert_reduce_fusion.2
  78.6 0.2 select_reduce_fusion.2
  78.7 1.3 compare_select_fusion.1
  80.1 0.1 concatenate.7.plan
  80.2 4.1 %copy-done.1 = f32[24,7,128,128]{3,2,1,0:T(8,128)S(1)} copy-done((f32[24,7,128,128]{3,2,1,0:T(8,128)S(1)}, f32[24,7,128,128]{3,2,1,0:T(8,128)}, u32[]{:S(2)}) %copy-start.1) | copy-done | bytes 11010072
  84.3 7.5 %near_op.2 = (f32[24,128,128]{2,1,0:T(8,128)S(1)}, bf16[168,128,256]{2,1,0:T(8,128)(2,1)S(1)}, f32[64,64]{1,0:T(8,128)S(1)}) custom-call(s32[1014]{0:T(1024)S(1)} %concatenate.7.plan, f32[168,128,128]{2,1,0:T(8,128)S(1)} %bitcast.24, f32[64,3072]{1,0:T(8,128)S(1)} %project.3.mid.prev.refs_1_.refs_2_), custom_call_target="tpu_custom_call" | custom-call | flops 2000000000 | bytes 12582912 | tf_op jit(solution)/shard_map/near_op/pallas_call | solution.py:144
  91.8 2.1 collective-permute-done.left
  93.9 5.8 %far_op.2 = (f32[64,3072]{1,0:T(8,128)S(1)}, f32[128,1,384]{2,1,0:T(1,128)S(1)}) custom-call(s32[1014]{0:T(1024)S(1)} %concatenate.7.plan, bf16[168,128,256]{2,1,0:T(8,128)(2,1)S(1)} %get-tuple-element.24.halves, f32[512,3072]{1,0:T(8,128)S(1)} %bitcast.19, f32[64,3072]{1,0:T(8,128)} %collective-permute-done.left, f32[64,3072]{1,0:T(8,128)} %collective-permute-done.1.right, ...), custom_call_target="tpu_custom_call" | custom-call | flops 2000000000 | bytes 20971520 | tf_op jit(solution)/shard_map/far_op/pallas_call | solution.py:164
  99.7 0.9 copy-done.12
  100.6 19.5 %all_to_all.30 = f32[128,1,384]{2,1,0:T(1,128)S(1)} all-to-all(f32[128,1,384]{2,1,0:T(1,128)S(1)} %get-tuple-element.27), channel_id=1, replica_groups=mesh['row'=4,'basis'=8,'rep'=4] {'row','basis','rep'}, dimensions={0} | all-to-all | bytes 393216 | tf_op jit(solution)/shard_map/all_to_all | solution.py:39
  120.0 0.2 reduce_sum.108
  120.2 0.8 broadcast_in_dim.81
  121.0 4.9 %all-to-all-start.3 = ((f32[128,1,384]{2,1,0:T(1,128)}), f32[128,1,384]{2,1,0:T(1,128)}, u32[]{:S(2)}, u32[]{:S(2)}) async-start(f32[128,1,384]{2,1,0:T(1,128)} %broadcast_in_dim.81), calls=%async_computation.3 | async-start | bytes 393216 | tf_op jit(solution)/shard_map/all_to_all | solution.py:41
  125.9 1.2 copy-done.5
  127.1 0.7 after_first.1.c3t
  127.8 8.5 %all-to-all-done.3 = f32[128,1,384]{2,1,0:T(1,128)} async-done(((f32[128,1,384]{2,1,0:T(1,128)}), f32[128,1,384]{2,1,0:T(1,128)}, u32[]{:S(2)}, u32[]{:S(2)}) %all-to-all-start.3) | async-done | bytes 196640 | tf_op jit(solution)/shard_map/all_to_all | solution.py:41
  136.3 0.9 copy.50
  137.3 1.4 copy-done.6
  138.6 3.4 %second.1 = (f32[64,512]{1,0:T(8,128)S(1)}, f32[64,128]{1,0:T(8,128)S(1)}, f32[192,512]{1,0:T(8,128)S(1)}) custom-call(f32[128,384]{1,0:T(8,128)S(1)} %bitcast.30, f32[512,512]{1,0:T(8,128)S(1)} %copy-done.6, f32[64,512]{1,0:T(8,128)S(1)} %after_first.1.c3t), custom_call_target="tpu_custom_call" | custom-call | flops 10000000000 | bytes 2097152 | tf_op jit(solution)/shard_map/second/pallas_call | solution.py:352
  142.1 1.9 project.4.mid.refs_1_
  144.0 0.4 collective-permute-start.2
  144.4 7.2 %collective-permute-start.3 = (f32[64,3072]{1,0:T(8,128)S(1)}, f32[64,3072]{1,0:T(8,128)S(1)}, u32[]{:S(2)}, u32[]{:S(2)}) collective-permute-start(f32[64,3072]{1,0:T(8,128)S(1)} %project.4.mid.refs_1_), channel_id=1, source_target_pairs={{1,0},{2,1},{3,2},{4,3},{5,4},{6,5},{7,6},{8,7},{9,8},{10,9},{11,1... | collective-permute-start | bytes 2359304 | tf_op jit(solution)/shard_map/ppermute | solution.py:376
  151.5 7.5 %near_op.3 = (f32[24,128,128]{2,1,0:T(8,128)S(1)}, bf16[168,128,256]{2,1,0:T(8,128)(2,1)S(1)}, f32[64,64]{1,0:T(8,128)S(1)}) custom-call(s32[1014]{0:T(1024)S(1)} %concatenate.7.plan, f32[168,128,128]{2,1,0:T(8,128)S(1)} %bitcast.27, f32[64,3072]{1,0:T(8,128)S(1)} %project.4.mid.refs_1_), custom_call_target="tpu_custom_call" | custom-call | flops 2000000000 | bytes 12582912 | tf_op jit(solution)/shard_map/near_op/pallas_call | solution.py:144
  159.0 10.2 %collective-permute-done.2.left = f32[64,3072]{1,0:T(8,128)S(1)} collective-permute-done((f32[64,3072]{1,0:T(8,128)S(1)}, f32[64,3072]{1,0:T(8,128)S(1)}, u32[]{:S(2)}, u32[]{:S(2)}) %collective-permute-start.2) | collective-permute-done | bytes 786464 | tf_op jit(solution)/shard_map/ppermute | solution.py:376
  169.2 5.1 %far_op.3 = (f32[64,3072]{1,0:T(8,128)S(1)}, f32[128,1,384]{2,1,0:T(1,128)S(1)}) custom-call(s32[1014]{0:T(1024)S(1)} %concatenate.7.plan, bf16[168,128,256]{2,1,0:T(8,128)(2,1)S(1)} %get-tuple-element.33.halves, f32[512,3072]{1,0:T(8,128)S(1)} %bitcast.21, f32[64,3072]{1,0:T(8,128)S(1)} %collective-permute-done.2.left, ...), custom_call_target="tpu_custom_call" | custom-call | flops 2000000000 | bytes 20971520 | tf_op jit(solution)/shard_map/far_op/pallas_call | solution.py:164
  174.3 0.9 copy-done.10
  175.1 19.1 %all_to_all.31 = f32[128,1,384]{2,1,0:T(1,128)S(1)} all-to-all(f32[128,1,384]{2,1,0:T(1,128)S(1)} %get-tuple-element.36), channel_id=1, replica_groups=mesh['row'=4,'basis'=8,'rep'=4] {'row','basis','rep'}, dimensions={0} | all-to-all | bytes 393216 | tf_op jit(solution)/shard_map/all_to_all | solution.py:39
  194.2 0.2 reduce_sum.109
  194.4 0.8 broadcast_in_dim.82
  195.2 5.2 %all-to-all-start.5 = ((f32[128,1,384]{2,1,0:T(1,128)}), f32[128,1,384]{2,1,0:T(1,128)}, u32[]{:S(2)}, u32[]{:S(2)}) async-start(f32[128,1,384]{2,1,0:T(1,128)} %broadcast_in_dim.82), calls=%async_computation.5 | async-start | bytes 393216 | tf_op jit(solution)/shard_map/all_to_all | solution.py:41
  200.4 1.2 copy-done.7
  201.6 0.9 after.1.c3
  202.6 8.3 %all-to-all-done.5 = f32[128,1,384]{2,1,0:T(1,128)} async-done(((f32[128,1,384]{2,1,0:T(1,128)}), f32[128,1,384]{2,1,0:T(1,128)}, u32[]{:S(2)}, u32[]{:S(2)}) %all-to-all-start.5) | async-done | bytes 196640 | tf_op jit(solution)/shard_map/all_to_all | solution.py:41
  210.8 0.9 copy.49
  211.8 1.2 copy-done.8
  213.0 8.5 %third.1 = (f32[64,512]{1,0:T(8,128)S(1)}, f32[64,192]{1,0:T(8,128)S(1)}, f32[2,64,64]{2,1,0:T(8,128)}, f32[2,64,64]{2,1,0:T(8,128)}) custom-call(f32[128,384]{1,0:T(8,128)S(1)} %bitcast.29, f32[512,512]{1,0:T(8,128)S(1)} %copy-done.8, f32[64,640]{1,0:T(8,128)S(1)} %after.1.c3, f32[192,512]{1,0:T(8,128)S(1)} %get-tuple-element.37.keep), custom_call_target="tpu_custom_call" | custom-call | flops 10000000000 | bytes 2097152 | tf_op jit(solution)/shard_map/third/pallas_call | solution.py:352
  221.6 2.9 %project.5 = f32[64,3072]{1,0:T(8,128)} custom-call(f32[64,512]{1,0:T(8,128)S(1)} %get-tuple-element.40.cs, f32[64,192]{1,0:T(8,128)S(1)} %get-tuple-element.41.cw, f32[512,3072]{1,0:T(8,128)S(1)} %bitcast.23, f32[64,3072]{1,0:T(8,128)S(1)} %copy-done.11, f32[64,3072]{1,0:T(8,128)S(1)} %copy-done.3, f32[64,3072]{1,0:T(8,128)S(1)} %project.3.mid.prev.refs_1_.refs_2_), custom_call_target="tpu_custom_call" | custom-call | tf_op jit(solution)/shard_map/project/pallas_call | solution.py:225
  (61 shorter events, 0.2 us)
Async XLA Ops:
  0.6 6.9 %copy-start = (f32[512,3072]{1,0:T(8,128)S(1)}, f32[512,3072]{1,0:T(8,128)}, u32[]{:S(2)}) copy-start(f32[512,3072]{1,0:T(8,128)} %stored.9) | copy-start | bytes 18874372
  0.6 8.7 %copy-start.9 = (f32[64,3072]{1,0:T(8,128)S(1)}, f32[64,3072]{1,0:T(8,128)}, u32[]{:S(2)}) copy-start(f32[64,3072]{1,0:T(8,128)} %refs_0_.1) | copy-start | bytes 2359300
  9.3 16.0 %copy-start.14 = (s32[24,7]{0,1:T(8,128)S(1)}, s32[24,7]{0,1:T(8,128)}, u32[]{:S(2)}) copy-start(s32[24,7]{0,1:T(8,128)} %param.6) | copy-start | bytes 2020
  9.3 16.2 %copy-start.15 = (s32[24]{0:T(128)S(1)}, s32[24]{0:T(128)}, u32[]{:S(2)}) copy-start(s32[24]{0:T(128)} %param.7) | copy-start | bytes 292
  13.8 27.8 %all-to-all-start = ((f32[128,1,1536]{2,1,0:T(1,128)}), f32[128,1,1536]{2,1,0:T(1,128)S(1)}, u32[]{:S(2)}, u32[]{:S(2)}) async-start(f32[128,1,1536]{2,1,0:T(1,128)} %copy.39), calls=%async_computation | async-start | bytes 1572864 | tf_op jit(solution)/shard_map/all_to_all | solution.py:39
  43.3 20.6 %all-to-all-start.1 = ((f32[128,1,1536]{2,1,0:T(1,128)}), f32[128,1,1536]{2,1,0:T(1,128)S(1)}, u32[]{:S(2)}, u32[]{:S(2)}) async-start(f32[128,1,1536]{2,1,0:T(1,128)} %broadcast_in_dim.80), calls=%async_computation.1 | async-start | bytes 1572864 | tf_op jit(solution)/shard_map/all_to_all | solution.py:41
  63.9 2.6 %slice-start = ((s8[6291456]{0:T(1024)(128)(4,1)}), s8[4194304]{0:T(1024)(128)(4,1)S(1)}, s32[]{:S(2)}) async-start(s8[6291456]{0:T(1024)(128)(4,1)} %bitcast.16), calls=%async_computation.6 | async-start | bytes 8388608
  64.0 3.2 %slice-start.1 = ((s8[6291456]{0:T(1024)(128)(4,1)}), s8[2097152]{0:T(1024)(128)(4,1)S(1)}, s32[]{:S(2)}) async-start(s8[6291456]{0:T(1024)(128)(4,1)} %bitcast.16), calls=%async_computation.7 | async-start | bytes 4194304
  64.7 4.3 %copy-start.4 = (f32[512,512]{1,0:T(8,128)}, f32[512,512]{1,0:T(8,128)S(1)}, u32[]{:S(2)}) copy-start(f32[512,512]{1,0:T(8,128)S(1)} %get-tuple-element.28.s) | copy-start | bytes 3145732
  69.0 24.8 %slice-start.2 = ((s8[6291456]{0:T(1024)(128)(4,1)}), s8[2097152]{0:T(1024)(128)(4,1)S(1)}, s32[]{:S(2)}) async-start(s8[6291456]{0:T(1024)(128)(4,1)} %bitcast.18), calls=%async_computation.8 | async-start | bytes 4194304
  69.0 24.8 %collective-permute-start = (f32[64,3072]{1,0:T(8,128)S(1)}, f32[64,3072]{1,0:T(8,128)}, u32[]{:S(2)}, u32[]{:S(2)}) collective-permute-start(f32[64,3072]{1,0:T(8,128)S(1)} %project.3.mid.prev.refs_1_.refs_2_), channel_id=1, source_target_pairs={{0,1},{1,2},{2,3},{3,4},{4,5},{5,6},{6,7},{7,8},{8,9},{9,10},{10,1... | collective-permute-start | bytes 2359304 | tf_op jit(solution)/shard_map/ppermute | solution.py:376
  69.5 24.4 %collective-permute-start.1 = (f32[64,3072]{1,0:T(8,128)S(1)}, f32[64,3072]{1,0:T(8,128)}, u32[]{:S(2)}, u32[]{:S(2)}) collective-permute-start(f32[64,3072]{1,0:T(8,128)S(1)} %project.3.mid.prev.refs_1_.refs_2_), channel_id=1, source_target_pairs={{1,0},{2,1},{3,2},{4,3},{5,4},{6,5},{7,6},{8,7},{9,8},{10,9},{11,1... | collective-permute-start | bytes 2359304 | tf_op jit(solution)/shard_map/ppermute | solution.py:376
  80.1 4.1 %copy-start.1 = (f32[24,7,128,128]{3,2,1,0:T(8,128)S(1)}, f32[24,7,128,128]{3,2,1,0:T(8,128)}, u32[]{:S(2)}) copy-start(f32[24,7,128,128]{3,2,1,0:T(8,128)} %param.5) | copy-start | bytes 33030148
  84.3 9.6 %slice-start.3 = ((s8[6291456]{0:T(1024)(128)(4,1)}), s8[4194304]{0:T(1024)(128)(4,1)S(1)}, s32[]{:S(2)}) async-start(s8[6291456]{0:T(1024)(128)(4,1)} %bitcast.18), calls=%async_computation.9 | async-start | bytes 8388608
  99.7 0.9 copy-start.12
  121.0 15.3 %all-to-all-start.3 = ((f32[128,1,384]{2,1,0:T(1,128)}), f32[128,1,384]{2,1,0:T(1,128)}, u32[]{:S(2)}, u32[]{:S(2)}) async-start(f32[128,1,384]{2,1,0:T(1,128)} %broadcast_in_dim.81), calls=%async_computation.3 | async-start | bytes 393216 | tf_op jit(solution)/shard_map/all_to_all | solution.py:41
  125.9 1.2 copy-start.5
  127.1 15.0 %slice-start.4 = ((s8[6291456]{0:T(1024)(128)(4,1)}), s8[2097152]{0:T(1024)(128)(4,1)S(1)}, s32[]{:S(2)}) async-start(s8[6291456]{0:T(1024)(128)(4,1)} %bitcast.20), calls=%async_computation.10 | async-start | bytes 4194304
  137.2 14.3 %slice-start.8 = ((s8[11010048]{0:T(1024)(128)(4,1)}), s8[4194304]{0:T(1024)(128)(4,1)S(1)}, s32[]{:S(2)}) async-start(s8[11010048]{0:T(1024)(128)(4,1)} %bitcast.25), calls=%async_computation.14 | async-start | bytes 8388608
  137.2 1.4 copy-start.6
  138.6 3.4 %slice-start.5 = ((s8[6291456]{0:T(1024)(128)(4,1)}), s8[4194304]{0:T(1024)(128)(4,1)S(1)}, s32[]{:S(2)}) async-start(s8[6291456]{0:T(1024)(128)(4,1)} %bitcast.20), calls=%async_computation.11 | async-start | bytes 8388608
  138.6 3.4 %copy-start.13 = (f32[64,3072]{1,0:T(8,128)S(1)}, f32[64,3072]{1,0:T(8,128)}, u32[]{:S(2)}) copy-start(f32[64,3072]{1,0:T(8,128)} %copy-done.12) | copy-start | bytes 2359300
  138.6 12.9 %slice-start.9 = ((s8[11010048]{0:T(1024)(128)(4,1)}), s8[4194304]{0:T(1024)(128)(4,1)S(1)}, s32[]{:S(2)}) async-start(s8[11010048]{0:T(1024)(128)(4,1)} %bitcast.25), calls=%async_computation.15 | async-start | bytes 8388608
  138.6 12.9 %slice-start.10 = ((s8[11010048]{0:T(1024)(128)(4,1)}), s8[2621440]{0:T(1024)(128)(4,1)S(1)}, s32[]{:S(2)}) async-start(s8[11010048]{0:T(1024)(128)(4,1)} %bitcast.25), calls=%async_computation.16 | async-start | bytes 5242880
  144.0 30.3 %copy-start.2 = (f32[64,3072]{1,0:T(8,128)}, f32[64,3072]{1,0:T(8,128)S(1)}, u32[]{:S(2)}) copy-start(f32[64,3072]{1,0:T(8,128)S(1)} %project.4.mid.refs_1_) | copy-start | bytes 2359300
  144.0 25.2 %collective-permute-start.2 = (f32[64,3072]{1,0:T(8,128)S(1)}, f32[64,3072]{1,0:T(8,128)S(1)}, u32[]{:S(2)}, u32[]{:S(2)}) collective-permute-start(f32[64,3072]{1,0:T(8,128)S(1)} %project.4.mid.refs_1_), channel_id=1, source_target_pairs={{0,1},{1,2},{2,3},{3,4},{4,5},{5,6},{6,7},{7,8},{8,9},{9,10},{10,1... | collective-permute-start | bytes 2359304 | tf_op jit(solution)/shard_map/ppermute | solution.py:376
  144.4 24.8 %collective-permute-start.3 = (f32[64,3072]{1,0:T(8,128)S(1)}, f32[64,3072]{1,0:T(8,128)S(1)}, u32[]{:S(2)}, u32[]{:S(2)}) collective-permute-start(f32[64,3072]{1,0:T(8,128)S(1)} %project.4.mid.refs_1_), channel_id=1, source_target_pairs={{1,0},{2,1},{3,2},{4,3},{5,4},{6,5},{7,6},{8,7},{9,8},{10,9},{11,1... | collective-permute-start | bytes 2359304 | tf_op jit(solution)/shard_map/ppermute | solution.py:376
  174.2 0.9 copy-start.10
  195.2 26.4 %slice-start.6 = ((s8[6291456]{0:T(1024)(128)(4,1)}), s8[2097152]{0:T(1024)(128)(4,1)S(1)}, s32[]{:S(2)}) async-start(s8[6291456]{0:T(1024)(128)(4,1)} %bitcast.22), calls=%async_computation.12 | async-start | bytes 4194304
  195.2 15.6 %all-to-all-start.5 = ((f32[128,1,384]{2,1,0:T(1,128)}), f32[128,1,384]{2,1,0:T(1,128)}, u32[]{:S(2)}, u32[]{:S(2)}) async-start(f32[128,1,384]{2,1,0:T(1,128)} %broadcast_in_dim.82), calls=%async_computation.5 | async-start | bytes 393216 | tf_op jit(solution)/shard_map/all_to_all | solution.py:41
  200.4 1.2 copy-start.7
  211.8 1.2 copy-start.8
  213.0 8.6 %slice-start.7 = ((s8[6291456]{0:T(1024)(128)(4,1)}), s8[4194304]{0:T(1024)(128)(4,1)S(1)}, s32[]{:S(2)}) async-start(s8[6291456]{0:T(1024)(128)(4,1)} %bitcast.22), calls=%async_computation.13 | async-start | bytes 8388608
  213.0 8.6 %copy-start.3 = (f32[64,3072]{1,0:T(8,128)S(1)}, f32[64,3072]{1,0:T(8,128)}, u32[]{:S(2)}) copy-start(f32[64,3072]{1,0:T(8,128)} %copy-done.2) | copy-start | bytes 2359300
  213.0 8.6 %copy-start.11 = (f32[64,3072]{1,0:T(8,128)S(1)}, f32[64,3072]{1,0:T(8,128)}, u32[]{:S(2)}) copy-start(f32[64,3072]{1,0:T(8,128)} %copy-done.10) | copy-start | bytes 2359300
